TPU v7x, 128 devices: a whole 4x4x4 slice. The times are simulated.
128 devices in a mesh: gx: 16 (over x_hi, z, core), gy: 8 (over y, x_lo).
Axes of the slice: x: 4 (x_hi: 2, x_lo: 2; x = x_hi * 2 + x_lo), y: 4, z: 4, core: 2. Of those that a mesh axis runs over, the one named last changes fastest.
Arguments:
- populations: float32 [19, 128, 128, 128], P(None, 'gx', 'gy'), may hold values from 0 to 1.25, as said below
- solid_mask: int32 [128, 128, 128], P('gx', 'gy'), may hold values 0 or 1
- wall_class: int32 [128, 128, 128], P('gx', 'gy'), may hold values from 0 to 7
- wall_table: float32 [8], replicated, may hold values from 0.2 to 0.9
- relax_rates: float32 [19], replicated, may hold values from 0.7 to 1.6
- pop_cotangent: float32 [19, 128, 128, 128], P(None, 'gx', 'gy'), may hold values from -6 to 6
Outputs:
- pop_adjoint: float32 [19, 128, 128, 128], P(None, 'gx', 'gy')
- density_adjoint: float32 [2, 128, 128, 128], P(None, 'gx', 'gy')
- wet_gradient: float32 [128, 128, 128], P('gx', 'gy')
Inputs may be any that keep to these rules, and one draw needn't show every extreme that they name: `populations`: every population is positive.
All inputs are finite; a program needn't handle non-finite values. No bound on the sum of `solid_mask` on one device may be relied on, other than what follows from the above.
Results may differ from a plain program's by a relative error of at most 0.00014.
Values sent between devices are 32-bit elements; how exact they have to be, the bound alone decides.
A program may use at most 64 MiB of HBM per device.

v0:
```python
import functools

import jax
import jax.numpy as jnp
from jax import lax
from jax.experimental import pallas as pl
from jax.experimental.pallas import tpu as pltpu
from jax.sharding import PartitionSpec as P

MESH = pl.DeviceIdType.MESH
VELOCITY = [
    (0, 0, 0),
    (1, 0, 0), (-1, 0, 0), (0, 1, 0), (0, -1, 0), (0, 0, 1), (0, 0, -1),
    (1, 1, 0), (-1, -1, 0), (1, -1, 0), (-1, 1, 0),
    (1, 0, 1), (-1, 0, -1), (1, 0, -1), (-1, 0, 1),
    (0, 1, 1), (0, -1, -1), (0, 1, -1), (0, -1, 1),
]
FACE_W, EDGE_W = 1.0 / 18.0, 1.0 / 36.0
AXES = (0, 1, 2)
PAIRS = ((0, 1), (0, 2), (1, 2))
CROSS = {(0, 1): 4, (0, 2): 5, (1, 2): 6}
QUAD = {(0, 1): 16, (0, 2): 17, (1, 2): 18}
CUBIC = {(0, 1): 10, (0, 2): 11, (1, 0): 12, (1, 2): 13, (2, 0): 14, (2, 1): 15}
EDGE = {(0, 1): 7, (0, 2): 11, (1, 2): 15}
ODD = (1, 2, 3, 10, 11, 12, 13, 14, 15)
OTHERS = {0: (1, 2), 1: (0, 2), 2: (0, 1)}
DIRS = ((-1, -1), (-1, 1), (1, -1), (1, 1), (-1, 0), (1, 0), (0, -1), (0, 1))
CLASSES = [(a, b) for a in (-1, 0, 1) for b in (-1, 0, 1)]
SLOT = {c: n for n, c in enumerate(CLASSES)}
MEMBERS = {c: [i for i, v in enumerate(VELOCITY) if v[:2] == c] for c in CLASSES}
H, B, Z = 8, 16, 128
Y0, Y1 = 8, 24
MID = slice(Y0, Y1)
ROWS = (16, 112, 104, 152, 48)


def quad(a, b):
    return QUAD[(min(a, b), max(a, b))]


def cross(a, b):
    return CROSS[(min(a, b), max(a, b))]


def roll_z(v, shift):
    return v if shift == 0 else pltpu.roll(v, shift % Z, v.ndim - 1)


def moments(f):
    m = [None] * 19
    s = [f[1 + 2 * a] + f[2 + 2 * a] for a in AXES]
    d = [f[1 + 2 * a] - f[2 + 2 * a] for a in AXES]
    for a, b in PAIRS:
        e = EDGE[a, b]
        al, ad = f[e] + f[e + 1], f[e] - f[e + 1]
        be, bd = f[e + 2] + f[e + 3], f[e + 2] - f[e + 3]
        m[CROSS[a, b]] = al - be
        m[QUAD[a, b]] = al + be
        m[CUBIC[a, b]] = ad + bd
        m[CUBIC[b, a]] = ad - bd
    for a in AXES:
        b, c = OTHERS[a]
        m[1 + a] = d[a] + (m[CUBIC[a, b]] + m[CUBIC[a, c]])
        m[7 + a] = s[a] + (m[quad(a, b)] + m[quad(a, c)])
    m[0] = (f[0] + s[0]) + (s[1] + s[2]) + (m[16] + m[17] + m[18])
    return m


def from_moments(p):
    f = [None] * 19
    for a in AXES:
        b, c = OTHERS[a]
        s = 0.5 * (p[7 + a] - (p[quad(a, b)] + p[quad(a, c)]))
        d = 0.5 * (p[1 + a] - (p[CUBIC[a, b]] + p[CUBIC[a, c]]))
        f[1 + 2 * a], f[2 + 2 * a] = s + d, s - d
    for a, b in PAIRS:
        e = EDGE[a, b]
        q, r = 0.25 * p[QUAD[a, b]], 0.25 * p[CROSS[a, b]]
        t, w = 0.25 * p[CUBIC[a, b]], 0.25 * p[CUBIC[b, a]]
        up, down, plus, minus = q + r, q - r, t + w, t - w
        f[e], f[e + 1], f[e + 2], f[e + 3] = up + plus, up - plus, down + minus, down - minus
    f[0] = p[0] - (p[7] + p[8] + p[9]) + (p[16] + p[17] + p[18])
    return f


def from_moments_t(lam):
    mu = [None] * 19
    mu[0] = lam[0]
    s = [0.5 * (lam[1 + 2 * a] + lam[2 + 2 * a]) for a in AXES]
    d = [0.5 * (lam[1 + 2 * a] - lam[2 + 2 * a]) for a in AXES]
    for a in AXES:
        mu[1 + a] = d[a]
        mu[7 + a] = s[a] - lam[0]
    for a, b in PAIRS:
        e = EDGE[a, b]
        al, ad = lam[e] + lam[e + 1], lam[e] - lam[e + 1]
        be, bd = lam[e + 2] + lam[e + 3], lam[e + 2] - lam[e + 3]
        mu[QUAD[a, b]] = 0.25 * (al + be) - s[a] - mu[7 + b]
        mu[CROSS[a, b]] = 0.25 * (al - be)
        mu[CUBIC[a, b]] = 0.25 * (ad + bd) - d[a]
        mu[CUBIC[b, a]] = 0.25 * (ad - bd) - d[b]
    return mu


def moments_t(nu):
    f = [None] * 19
    f[0] = nu[0]
    for a in AXES:
        s = nu[0] + nu[7 + a]
        f[1 + 2 * a], f[2 + 2 * a] = s + nu[1 + a], s - nu[1 + a]
    for a, b in PAIRS:
        e = EDGE[a, b]
        even = (nu[0] + nu[7 + a]) + (nu[7 + b] + nu[QUAD[a, b]])
        up, down = even + nu[CROSS[a, b]], even - nu[CROSS[a, b]]
        p, q = nu[1 + a] + nu[CUBIC[a, b]], nu[1 + b] + nu[CUBIC[b, a]]
        f[e], f[e + 1], f[e + 2], f[e + 3] = up + (p + q), up - (p + q), down + (p - q), down - (p - q)
    return f


def collide(f, psi, pull, inv, solid, rate):
    m = moments(f)
    rho = m[0]
    force = [5.0 * psi * g for g in pull]
    u = [(m[1 + a] + 0.5 * force[a]) * inv for a in AXES]
    n = [m[1 + a] - 0.5 * force[a] for a in AXES]
    p = [None] * 19
    p[0] = rho
    w = [u[a] * n[a] for a in AXES]
    t = [u[a] * force[a] for a in AXES]
    third = rho * (1.0 / 3.0)
    ninth = rho * (1.0 / 9.0)
    for a in AXES:
        p[1 + a] = m[1 + a] + force[a]
        k = 7 + a
        p[k] = m[k] + rate[k] * (third + w[a] - m[k]) + 2.0 * t[a]
    m3 = [m[1 + a] * (1.0 / 3.0) for a in AXES]
    f3 = [force[a] * (1.0 / 3.0) for a in AXES]
    for (a, b), k in CUBIC.items():
        p[k] = m[k] + rate[k] * (m3[a] - m[k]) + f3[a]
    w3 = [(1.0 / 3.0) * v for v in w]
    t3 = [(1.0 / 3.0) * v for v in t]
    for a, b in PAIRS:
        c = 3 - a - b
        k = CROSS[a, b]
        p[k] = m[k] + rate[k] * (0.5 * (u[b] * n[a] + u[a] * n[b]) - m[k]) + (u[a] * force[b] + u[b] * force[a])
        k = QUAD[a, b]
        p[k] = (
            m[k]
            + rate[k] * (ninth + (w3[a] + w3[b]) - 0.5 * w3[c] - m[k])
            + (2.0 * (t3[a] + t3[b]) - t3[c])
        )
    for k in range(1, 19):
        p[k] = jnp.where(solid, -m[k] if k in ODD else m[k], p[k])
    return from_moments(p), u, force


def collide_adjoint(lam, u, force, inv, solid, rate):
    mu = from_moments_t(lam)
    e, nu, g = [None] * 19, [None] * 19, [None] * 19
    for k in (0,) + tuple(range(4, 19)):
        e[k] = rate[k] * mu[k]
        nu[k] = mu[k] - e[k]
        g[k] = mu[k] - 0.5 * e[k]

    def diagonal(v):
        out = []
        for a in AXES:
            b, c = OTHERS[a]
            out.append(2.0 * v[7 + a] + (2.0 / 3.0) * (v[quad(a, b)] + v[quad(a, c)]) - (1.0 / 3.0) * v[quad(b, c)])
        return out

    def times(diag, v, x):
        out = []
        for a in AXES:
            b, c = OTHERS[a]
            out.append(diag[a] * x[a] + v[cross(a, b)] * x[b] + v[cross(a, c)] * x[c])
        return out

    ed, gd = diagonal(e), diagonal(g)
    eu, gu, gf = times(ed, e, u), times(gd, g, u), times(gd, g, force)
    fbar = []
    for a in AXES:
        b, c = OTHERS[a]
        jbar = (1.0 / 3.0) * (e[CUBIC[a, b]] + e[CUBIC[a, c]]) + eu[a] + gf[a] * inv
        cbar = mu[1 + a] + (1.0 / 3.0) * (g[CUBIC[a, b]] + g[CUBIC[a, c]]) + gu[a]
        nu[1 + a] = mu[1 + a] + jbar
        fbar.append(jnp.where(solid, 0.0, cbar + 0.5 * jbar))
    rho_bar = (
        e[0]
        + (1.0 / 3.0) * (e[7] + e[8] + e[9])
        + (1.0 / 9.0) * (e[16] + e[17] + e[18])
        - 0.5 * (u[0] * eu[0] + u[1] * eu[1] + u[2] * eu[2])
        - (force[0] * gu[0] + force[1] * gu[1] + force[2] * gu[2]) * inv
    )
    for k in range(19):
        nu[k] = jnp.where(solid, -mu[k] if k in ODD else mu[k], nu[k])
    return nu, fbar, jnp.where(solid, 0.0, rho_bar)


def neighbour_pull(ext, x):
    at = {(a, b): ext[x + 1 + a, Y0 + b : Y1 + b, :] for a, b in CLASSES}
    dx, dy = at[1, 0] - at[-1, 0], at[0, 1] - at[0, -1]
    main, other = at[1, 1] - at[-1, -1], at[1, -1] - at[-1, 1]
    total = FACE_W * at[0, 0] + EDGE_W * ((at[1, 0] + at[-1, 0]) + (at[0, 1] + at[0, -1]))
    gx = FACE_W * dx + EDGE_W * (main + other + (roll_z(dx, 1) + roll_z(dx, -1)))
    gy = FACE_W * dy + EDGE_W * (main - other + (roll_z(dy, 1) + roll_z(dy, -1)))
    return [gx, gy, roll_z(total, -1) - roll_z(total, 1)]


def spread_classes(p):
    px, py, pz = p
    up, down = roll_z(pz, 1), roll_z(pz, -1)
    side = {0: px, 1: py}
    turned = {a: EDGE_W * (roll_z(v, 1) + roll_z(v, -1)) + FACE_W * v for a, v in side.items()}
    lift = EDGE_W * (up - down)
    both, apart = EDGE_W * (px + py), EDGE_W * (px - py)
    return {
        (0, 0): FACE_W * (up - down),
        (1, 0): turned[0] + lift, (-1, 0): lift - turned[0],
        (0, 1): turned[1] + lift, (0, -1): lift - turned[1],
        (1, 1): both, (-1, -1): -both, (1, -1): apart, (-1, 1): -apart,
    }


def gather(ext, i, x, orient):
    cx, cy, _ = VELOCITY[i]
    return ext[i, x + 1 - orient * cx, Y0 - orient * cy : Y1 - orient * cy, :]


def class_sum(q, x):
    total = None
    for c in CLASSES:
        v = q[SLOT[c], x + 1 - c[0], Y0 - c[1] : Y1 - c[1], :]
        total = v if total is None else total + v
    return total


def chosen(d, orient):
    return [i for i, v in enumerate(VELOCITY) if all(d[n] == 0 or v[n] == orient * d[n] for n in (0, 1))]


def chosen_classes(d):
    return [c for c in CLASSES if all(d[n] == 0 or c[n] == d[n] for n in (0, 1))]


def edge_of(d):
    return (1 if d[0] < 0 else H), (Y0 if d[1] < 0 else Y1 - 1)


def halo_of(d):
    return (0 if d[0] > 0 else H + 1), (Y0 - 1 if d[1] > 0 else Y1)


def column(ext, y, shift=0):
    return jnp.concatenate([ext[1 + x + shift, y : y + 1, :] for x in range(H)], axis=0)


def pack(sb, k, place, ext):
    d = DIRS[k]
    ex, ey = edge_of(d)
    if d[1] == 0:
        sb[k, place * B : (place + 1) * B, :] = ext[ex, MID, :]
    elif d[0] == 0:
        for x in range(H):
            sb[k, place * H + x : place * H + x + 1, :] = ext[1 + x, ey : ey + 1, :]
    else:
        sb[k, place : place + 1, :] = ext[ex, ey : ey + 1, :]


def unpack(rb, k, place, ext):
    d = DIRS[k]
    hx, hy = halo_of(d)
    if d[1] == 0:
        ext[hx, MID, :] = rb[k, place * B : (place + 1) * B, :]
    elif d[0] == 0:
        for x in range(H):
            ext[1 + x, hy : hy + 1, :] = rb[k, place * H + x : place * H + x + 1, :]
    else:
        ext[hx, hy : hy + 1, :] = rb[k, place : place + 1, :]


def shifted(v, step):
    rows = v.shape[0]
    index = lax.broadcasted_iota(jnp.int32, v.shape, 0)
    return jnp.where(index == (0 if step > 0 else rows - 1), 0.0, pltpu.roll(v, step % rows, 0))


def pack_partial(sb, k, place, q):
    d = DIRS[k]
    ex, ey = edge_of(d)
    if d[1] == 0:
        t = {c: q[SLOT[0, c], ex, MID, :] + q[SLOT[d[0], c], ex - d[0], MID, :] for c in (-1, 0, 1)}
        at, size = place * B, B
    elif d[0] == 0:
        t = {c: column(q.at[SLOT[c, 0]], ey) + column(q.at[SLOT[c, d[1]]], ey - d[1]) for c in (-1, 0, 1)}
        at, size = place * H, H
    else:
        def one(c, x, y):
            return q[SLOT[c], x, y : y + 1, :]

        dx, dy = d
        sb[k, place : place + 1, :] = (
            one((0, 0), ex, ey) + one((dx, 0), ex - dx, ey) + one((0, dy), ex, ey - dy) + one(d, ex - dx, ey - dy)
        )
        sb[k, place + 1 : place + 2, :] = one((dx, 0), ex, ey) + one(d, ex, ey - dy)
        sb[k, place + 2 : place + 3, :] = one((0, dy), ex, ey) + one(d, ex - dx, ey)
        return
    sb[k, at : at + size, :] = t[0] + shifted(t[1], 1) + shifted(t[-1], -1)
    sb[k, at + size : at + size + 1, :] = t[-1][0:1, :]
    sb[k, at + size + 1 : at + size + 2, :] = t[1][size - 1 : size, :]


def border_sum(rb, places, q, out):
    at = {d: n for n, d in enumerate(DIRS)}
    for dx in (-1, 1):
        hx, _ = halo_of((dx, 0))
        ex, _ = edge_of((-dx, 0))
        k = at[dx, 0]
        n = places[k] * B
        total = rb[k, n : n + B, :]
        for c in (-1, 0, 1):
            total = total + q[SLOT[-dx, c], ex, Y0 - c : Y1 - c, :]
        out[hx, MID, :] = total
        for dy in (-1, 1):
            kc = at[dx, dy]
            _, ey = edge_of((0, -dy))
            out[hx, ey : ey + 1, :] += rb[kc, places[kc] + 2 : places[kc] + 3, :]
    for dy in (-1, 1):
        _, hy = halo_of((0, dy))
        _, ey = edge_of((0, -dy))
        k = at[0, dy]
        n = places[k] * H
        for x in range(H):
            total = rb[k, n + x : n + x + 1, :]
            for c in (-1, 0, 1):
                total = total + q[SLOT[c, -dy], x + 1 - c, ey : ey + 1, :]
            for dx in (-1, 1):
                if x == (0 if dx > 0 else H - 1):
                    kc = at[dx, dy]
                    total = total + rb[kc, places[kc] + 1 : places[kc] + 2, :]
            out[1 + x, hy : hy + 1, :] = total
    for dx in (-1, 1):
        for dy in (-1, 1):
            kc, kx, ky = at[dx, dy], at[dx, 0], at[0, dy]
            hx, hy = halo_of((dx, dy))
            ex, ey = edge_of((-dx, -dy))
            nx = places[kx] * B + B + (0 if dy > 0 else 1)
            ny = places[ky] * H + H + (0 if dx > 0 else 1)
            out[hx, hy : hy + 1, :] = (
                rb[kc, places[kc] : places[kc] + 1, :]
                + q[SLOT[-dx, -dy], ex, ey : ey + 1, :]
                + rb[kx, nx : nx + 1, :]
                + rb[ky, ny : ny + 1, :]
            )


def rows_of(k, fields, ends):
    d = DIRS[k]
    if d[1] == 0:
        return fields * B + (B + 8 if ends else 0)
    if d[0] == 0:
        return fields * H + (H + 8 if ends else 0)
    return 8


def kernel(
    nx, ny,
    table, rates, pops_hbm, mask_hbm, class_hbm, cot_hbm, base_hbm, extra_hbm,
    pops, cot, mask, wall_class, state, base_out, extra,
    psi_ext, solid_ext, wall_ext, e2_ext, sum_ext, d_ext, q_ext, cot_ext, post_ext, base_ext,
    s0, s1, s2, s3, s4, r0, r1, r2, r3, r4,
    send_sem, recv_sem, local_sem,
):
    gx, gy = lax.axis_index("gx"), lax.axis_index("gy")
    sends, recvs = (s0, s1, s2, s3, s4), (r0, r1, r2, r3, r4)

    def device(d):
        return (lax.rem(gx + (d[0] + nx), nx), lax.rem(gy + (d[1] + ny), ny))

    barrier = pltpu.get_barrier_semaphore()
    for d in DIRS:
        pl.semaphore_signal(barrier, inc=1, device_id=device(d), device_id_type=MESH)

    loads = [
        pltpu.make_async_copy(src, dst, local_sem.at[n])
        for n, (src, dst) in enumerate(
            ((pops_hbm, pops), (mask_hbm, mask), (class_hbm, wall_class), (cot_hbm, cot))
        )
    ]
    for c in loads:
        c.start()

    def start(r, fields, ends=False):
        copies = []
        for k, d in enumerate(DIRS):
            rows = pl.ds(0, rows_of(k, fields, ends))
            c = pltpu.make_async_remote_copy(
                src_ref=sends[r].at[k, rows], dst_ref=recvs[r].at[k, rows],
                send_sem=send_sem.at[r, k], recv_sem=recv_sem.at[r, k],
                device_id=device(d), device_id_type=MESH,
            )
            c.start()
            copies.append(c)
        return copies

    def finish(copies):
        for c in copies:
            c.wait()

    def each_row(body):
        def step(x, carry):
            body(x)
            return carry

        lax.fori_loop(0, H, step, 0)

    rate = [rates[k] for k in range(19)]

    for c in loads[:3]:
        c.wait()

    def prepare(x):
        f = [pops[i, x] for i in range(19)]
        rho = f[0]
        for i in range(1, 19):
            rho = rho + f[i]
        solid = mask[x] == 1
        kind = wall_class[x]
        wall = jnp.full(rho.shape, table[0], jnp.float32)
        for n in range(1, 8):
            wall = jnp.where(kind == n, table[n], wall)
        fade = jnp.exp(-rho)
        psi_ext[x + 1, MID, :] = jnp.where(solid, wall, 1.0 - fade)
        solid_ext[x + 1, MID, :] = jnp.where(solid, 1.0, 0.0)
        wall_ext[x + 1, MID, :] = wall
        state[0, x] = 1.0 / rho
        state[11, x] = jnp.where(solid, 0.0, fade)

    each_row(prepare)
    for k in range(8):
        pack(s0, k, 0, psi_ext)

    loads[3].wait()

    def turn(x):
        for i, c in enumerate(VELOCITY):
            cot_ext[i, x + 1, MID, :] = roll_z(cot[i, x], -c[2])

    each_row(turn)
    for k, d in enumerate(DIRS):
        ids = chosen(d, -1)
        for n, i in enumerate(ids):
            pack(s1, k, n, cot_ext.at[i])
        pack(s1, k, len(ids), solid_ext)
        pack(s1, k, len(ids) + 1, wall_ext)

    pl.semaphore_wait(barrier, len(DIRS))
    first = start(0, 1)
    early = start(1, 7)
    finish(first)
    for k in range(8):
        unpack(r0, k, 0, psi_ext)

    def forward(x):
        psi = psi_ext[x + 1, MID, :]
        pull = neighbour_pull(psi_ext, x)
        post, u, force = collide([pops[i, x] for i in range(19)], psi, pull, state[0, x], mask[x] == 1, rate)
        post = [roll_z(v, c[2]) for v, c in zip(post, VELOCITY)]
        for i in range(19):
            post_ext[i, x + 1, MID, :] = post[i]
        for c in CLASSES:
            total = post[MEMBERS[c][0]]
            for i in MEMBERS[c][1:]:
                total = total + post[i]
            q_ext[SLOT[c], x + 1, MID, :] = total
        for a in AXES:
            state[1 + a, x] = u[a]
            state[4 + a, x] = force[a]
            state[7 + a, x] = pull[a]
        state[10, x] = psi

    each_row(forward)
    places = []
    for k, d in enumerate(DIRS):
        ids = chosen(d, 1)
        for n, i in enumerate(ids):
            pack(s2, k, n, post_ext.at[i])
        pack_partial(s2, k, len(ids), q_ext)
        places.append(len(ids))
    second = start(2, 5, True)
    finish(early)
    for k, d in enumerate(DIRS):
        ids = chosen(d, -1)
        for n, i in enumerate(ids):
            unpack(r1, k, n, cot_ext.at[i])
        unpack(r1, k, len(ids), solid_ext)
        unpack(r1, k, len(ids) + 1, wall_ext)
    finish(second)

    for k, d in enumerate(DIRS):
        for n, i in enumerate(chosen(d, 1)):
            unpack(r2, k, n, post_ext.at[i])
    for d in DIRS:
        hx, hy = halo_of(d)
        for c in chosen_classes(d):
            if d[1] == 0:
                where = [(hx, MID)]
            elif d[0] == 0:
                where = [(1 + x, slice(hy, hy + 1)) for x in range(H)]
            else:
                where = [(hx, slice(hy, hy + 1))]
            for x, y in where:
                total = post_ext[MEMBERS[c][0], x, y, :]
                for i in MEMBERS[c][1:]:
                    total = total + post_ext[i, x, y, :]
                q_ext[SLOT[c], x, y, :] = total
    border_sum(r2, places, q_ext, sum_ext)

    def density(x):
        sum_ext[x + 1, MID, :] = class_sum(q_ext, x)

    each_row(density)

    def potential(x, carry):
        solid = solid_ext[x] > 0.5
        fade = jnp.exp(-sum_ext[x])
        psi_ext[x] = jnp.where(solid, wall_ext[x], 1.0 - fade)
        e2_ext[x] = jnp.where(solid, 0.0, fade)
        return carry

    lax.fori_loop(0, H + 2, potential, 0)

    def spread_out(fbar, psi, x):
        p = [5.0 * psi * v for v in fbar]
        for c, v in spread_classes(p).items():
            q_ext[SLOT[c], x + 1, MID, :] = v

    def backward_second(x):
        rho = sum_ext[x + 1, MID, :]
        inv = 1.0 / rho
        psi = psi_ext[x + 1, MID, :]
        solid = mask[x] == 1
        pull = neighbour_pull(psi_ext, x)
        force = [5.0 * psi * g for g in pull]
        f = [gather(post_ext, i, x, 1) for i in range(19)]
        u = []
        for a in AXES:
            m = None
            for i, c in enumerate(VELOCITY):
                if c[a] == 1:
                    m = f[i] if m is None else m + f[i]
            for i, c in enumerate(VELOCITY):
                if c[a] == -1:
                    m = m - f[i]
            u.append((m + 0.5 * force[a]) * inv)
        lam = [gather(cot_ext, i, x, -1) for i in range(19)]
        nu, fbar, rho_bar = collide_adjoint(lam, u, force, inv, solid, rate)
        local = rho_bar + e2_ext[x + 1, MID, :] * (
            5.0 * (pull[0] * fbar[0] + pull[1] * fbar[1] + pull[2] * fbar[2])
        )
        extra[2, x] = local
        nu[0] = nu[0] + local
        for i, v in enumerate(moments_t(nu)):
            base_ext[i, x + 1, MID, :] = roll_z(v, -VELOCITY[i][2])
        spread_out(fbar, psi, x)

    each_row(backward_second)
    places = []
    for k, d in enumerate(DIRS):
        ids, cs = chosen(d, -1), chosen_classes(d)
        for n, i in enumerate(ids):
            pack(s3, k, n, base_ext.at[i])
        for n, c in enumerate(cs):
            pack(s3, k, len(ids) + n, q_ext.at[SLOT[c]])
        pack_partial(s3, k, len(ids) + len(cs), q_ext)
        places.append(len(ids) + len(cs))
    finish(start(3, 8, True))
    for k, d in enumerate(DIRS):
        ids, cs = chosen(d, -1), chosen_classes(d)
        for n, i in enumerate(ids):
            unpack(r3, k, n, base_ext.at[i])
        for n, c in enumerate(cs):
            unpack(r3, k, len(ids) + n, q_ext.at[SLOT[c]])
    border_sum(r3, places, q_ext, sum_ext)

    def spread_second(x):
        total = class_sum(q_ext, x)
        sum_ext[x + 1, MID, :] = total
        extra[2, x] += e2_ext[x + 1, MID, :] * total
        extra[3, x] = jnp.where(mask[x] == 1, total, 0.0)

    each_row(spread_second)

    def shift_second(x, carry):
        v = e2_ext[x] * sum_ext[x]
        for c in (-1, 0, 1):
            d_ext[c + 1, x] = roll_z(v, -c)
        return carry

    lax.fori_loop(0, H + 2, shift_second, 0)

    def backward_first(x):
        solid = mask[x] == 1
        inv, psi = state[0, x], state[10, x]
        u = [state[1 + a, x] for a in AXES]
        force = [state[4 + a, x] for a in AXES]
        lam = []
        for i, c in enumerate(VELOCITY):
            more = d_ext[c[2] + 1, x + 1 + c[0], Y0 + c[1] : Y1 + c[1], :]
            lam.append(gather(base_ext, i, x, -1) + more)
        nu, fbar, rho_bar = collide_adjoint(lam, u, force, inv, solid, rate)
        local = rho_bar + state[11, x] * (
            5.0 * (state[7, x] * fbar[0] + state[8, x] * fbar[1] + state[9, x] * fbar[2])
        )
        extra[1, x] = local
        nu[0] = nu[0] + local
        for i, v in enumerate(moments_t(nu)):
            base_out[i, x] = v
        spread_out(fbar, psi, x)

    each_row(backward_first)
    for k, d in enumerate(DIRS):
        for n, c in enumerate(chosen_classes(d)):
            pack(s4, k, n, q_ext.at[SLOT[c]])
    last = start(4, 3)
    store = pltpu.make_async_copy(base_out, base_hbm, local_sem.at[4])
    store.start()
    finish(last)
    for k, d in enumerate(DIRS):
        for n, c in enumerate(chosen_classes(d)):
            unpack(r4, k, n, q_ext.at[SLOT[c]])

    def spread_first(x):
        total = class_sum(q_ext, x)
        change = state[11, x] * total
        extra[0, x] = change
        extra[1, x] += change
        extra[3, x] += jnp.where(mask[x] == 1, total, 0.0)

    each_row(spread_first)
    rest = pltpu.make_async_copy(extra, extra_hbm, local_sem.at[5])
    rest.start()
    rest.wait()
    store.wait()


def body(populations, solid_mask, wall_class, wall_table, relax_rates, pop_cotangent):
    f32 = jnp.float32
    nx, ny = lax.axis_size("gx"), lax.axis_size("gy")
    block = (H, B, Z)
    ext = (H + 2, 32, Z)
    anywhere = pl.BlockSpec(memory_space=pl.ANY)
    scalars = pl.BlockSpec(memory_space=pltpu.SMEM)
    vmem = pltpu.VMEM
    base, extra = pl.pallas_call(
        functools.partial(kernel, nx, ny),
        out_shape=(
            jax.ShapeDtypeStruct((19,) + block, f32),
            jax.ShapeDtypeStruct((4,) + block, f32),
        ),
        in_specs=[scalars, scalars] + [anywhere] * 4,
        out_specs=(anywhere, anywhere),
        scratch_shapes=[
            vmem((19,) + block, f32),
            vmem((19,) + block, f32),
            vmem(block, jnp.int32),
            vmem(block, jnp.int32),
            vmem((12,) + block, f32),
            vmem((19,) + block, f32),
            vmem((4,) + block, f32),
            vmem(ext, f32), vmem(ext, f32), vmem(ext, f32), vmem(ext, f32), vmem(ext, f32),
            vmem((3,) + ext, f32),
            vmem((9,) + ext, f32),
            vmem((19,) + ext, f32),
            vmem((19,) + ext, f32),
            vmem((19,) + ext, f32),
        ]
        + [vmem((8, n, Z), f32) for n in ROWS] * 2
        + [
            pltpu.SemaphoreType.DMA((5, 8)),
            pltpu.SemaphoreType.DMA((5, 8)),
            pltpu.SemaphoreType.DMA((6,)),
        ],
        compiler_params=pltpu.CompilerParams(
            collective_id=0, has_side_effects=True, vmem_limit_bytes=48 * 2**20
        ),
    )(wall_table, relax_rates, populations, solid_mask, wall_class, pop_cotangent)
    return base + extra[0][None], extra[1:3], extra[3]


def solution(mesh):
    in_specs = (
        P(None, "gx", "gy", None),
        P("gx", "gy", None),
        P("gx", "gy", None),
        P(),
        P(),
        P(None, "gx", "gy", None),
    )
    out_specs = (P(None, "gx", "gy", None), P(None, "gx", "gy", None), P("gx", "gy", None))
    return jax.shard_map(body, mesh=mesh, in_specs=in_specs, out_specs=out_specs, check_vma=False)
```

profile of v0, /device:TPU:0, one launch (start us, length us, event | category | flops | bytes accessed | tf_op | source)
XLA Modules:
  0.0 44.6 jit_solution(6959875388242989664)
XLA Ops:
  0.6 0.0 copy-start
  0.6 1.3 %copy-done = f32[19,8,16,128]{3,2,1,0:T(8,128)S(1)} copy-done((f32[19,8,16,128]{3,2,1,0:T(8,128)S(1)}, f32[19,8,16,128]{3,2,1,0:T(8,128)}, u32[]{:S(2)}) %copy-start) | copy-done | bytes 1245208
  1.9 0.0 copy-start.1
  1.9 1.3 %copy-done.1 = f32[19,8,16,128]{3,2,1,0:T(8,128)S(1)} copy-done((f32[19,8,16,128]{3,2,1,0:T(8,128)S(1)}, f32[19,8,16,128]{3,2,1,0:T(8,128)}, u32[]{:S(2)}) %copy-start.1) | copy-done | bytes 1245208
  3.2 0.0 copy-start.2
  3.2 0.8 %copy-done.2 = s32[8,16,128]{2,1,0:T(8,128)S(1)} copy-done((s32[8,16,128]{2,1,0:T(8,128)S(1)}, s32[8,16,128]{2,1,0:T(8,128)}, u32[]{:S(2)}) %copy-start.2) | copy-done | bytes 65560
  4.1 0.0 copy-start.3
  4.1 0.8 %copy-done.3 = s32[8,16,128]{2,1,0:T(8,128)S(1)} copy-done((s32[8,16,128]{2,1,0:T(8,128)S(1)}, s32[8,16,128]{2,1,0:T(8,128)}, u32[]{:S(2)}) %copy-start.3) | copy-done | bytes 65560
  4.9 0.0 copy-start.4
  4.9 0.7 %copy-done.4 = f32[8]{0:T(128)S(1)} copy-done((f32[8]{0:T(128)S(1)}, f32[8]{0:T(128)}, u32[]{:S(2)}) %copy-start.4) | copy-done | bytes 56
  5.6 0.0 copy-start.5
  5.6 0.7 %copy-done.5 = f32[19]{0:T(128)S(1)} copy-done((f32[19]{0:T(128)S(1)}, f32[19]{0:T(128)}, u32[]{:S(2)}) %copy-start.5) | copy-done | bytes 100
  6.2 35.9 %shard_map.85 = (f32[19,8,16,128]{3,2,1,0:T(8,128)S(1)}, f32[4,8,16,128]{3,2,1,0:T(8,128)S(1)}) custom-call(f32[8]{0:T(128)S(1)} %copy-done.4, f32[19]{0:T(128)S(1)} %copy-done.5, f32[19,8,16,128]{3,2,1,0:T(8,128)S(1)} %copy-done, s32[8,16,128]{2,1,0:T(8,128)S(1)} %copy-done.2, s32[8,16,128]{2,1,0:T(8,128)S(1)} %copy-done.3, f32[19,8,16,128]{3,2,1,0:T(8,128)S(1)} %copy-done.1), custom_call_target="tpu_custom_call" | custom-call | tf_op jit(solution)/shard_map/pallas_call | solution.py:655
  42.1 0.7 %slice.10 = f32[2,8,16,128]{3,2,1,0:T(8,128)} slice(f32[4,8,16,128]{3,2,1,0:T(8,128)S(1)} %get-tuple-element.6), slice={[1:3], [0:8], [0:16], [0:128]} | slice | bytes 262144 | tf_op jit(solution)/shard_map/slice | solution.py:688
  42.8 0.6 %slice_bitcast_fusion = (f32[8,16,128]{2,1,0:T(8,128)}, f32[8,16,128]{2,1,0:T(8,128)S(1)}) fusion(f32[4,8,16,128]{3,2,1,0:T(8,128)S(1)} %get-tuple-element.6), kind=kLoop, calls=%fused_computation.1 | loop fusion | bytes 262144 | tf_op jit(solution)/shard_map/squeeze | solution.py:688
  43.4 1.2 %broadcast_add_fusion = f32[19,8,16,128]{3,2,1,0:T(8,128)} fusion(f32[19,8,16,128]{3,2,1,0:T(8,128)S(1)} %get-tuple-element.5, f32[8,16,128]{2,1,0:T(8,128)S(1)} %get-tuple-element.8), kind=kLoop, calls=%fused_computation | loop fusion | flops 311296 | bytes 2555904 | tf_op jit(solution)/shard_map/add | solution.py:688
Async XLA Ops:
  0.6 1.3 %copy-start = (f32[19,8,16,128]{3,2,1,0:T(8,128)S(1)}, f32[19,8,16,128]{3,2,1,0:T(8,128)}, u32[]{:S(2)}) copy-start(f32[19,8,16,128]{3,2,1,0:T(8,128)} %pops_hbm.1) | copy-start | bytes 3735556
  1.9 1.3 %copy-start.1 = (f32[19,8,16,128]{3,2,1,0:T(8,128)S(1)}, f32[19,8,16,128]{3,2,1,0:T(8,128)}, u32[]{:S(2)}) copy-start(f32[19,8,16,128]{3,2,1,0:T(8,128)} %cot_hbm.1) | copy-start | bytes 3735556
  3.2 0.8 %copy-start.2 = (s32[8,16,128]{2,1,0:T(8,128)S(1)}, s32[8,16,128]{2,1,0:T(8,128)}, u32[]{:S(2)}) copy-start(s32[8,16,128]{2,1,0:T(8,128)} %mask_hbm.1) | copy-start | bytes 196612
  4.1 0.8 %copy-start.3 = (s32[8,16,128]{2,1,0:T(8,128)S(1)}, s32[8,16,128]{2,1,0:T(8,128)}, u32[]{:S(2)}) copy-start(s32[8,16,128]{2,1,0:T(8,128)} %class_hbm.1) | copy-start | bytes 196612
  4.9 0.7 %copy-start.4 = (f32[8]{0:T(128)S(1)}, f32[8]{0:T(128)}, u32[]{:S(2)}) copy-start(f32[8]{0:T(128)} %table.1) | copy-start | bytes 100
  5.6 0.7 %copy-start.5 = (f32[19]{0:T(128)S(1)}, f32[19]{0:T(128)}, u32[]{:S(2)}) copy-start(f32[19]{0:T(128)} %rates.1) | copy-start | bytes 232
where the time goes:
time: 44.8 us; the launch traced here: 44.6 us
  Pallas kernels  35.9 us (80%)
  local copies, waits for them, and re-layouts  6.87 us (15%)
  other arithmetic  1.15 us (3%)
  between operations  0.65 us (1%)
    pallas_call x1, Pallas kernels, body(): pl.pallas_call(functools.partial(kernel, nx, ny), out_shape=(jax.ShapeDty...  35.9 us
    unnamed x12, local copies, waits for them, and re-layouts  5.57 us
    add x1, other arithmetic, body(): return (base + extra[0][None], extra[1:3], extra[3])  1.15 us

commit v1 on v0

--- a/solution.py
+++ b/solution.py
@@ -251,8 +251,16 @@
     return (0 if d[0] > 0 else H + 1), (Y0 - 1 if d[1] > 0 else Y1)
 
 
+def strip(y, shift=0):
+    return pl.ds((1 + shift) * 32 + y, H, stride=32)
+
+
+def flat(ext):
+    return ext.reshape((H + 2) * 32, Z)
+
+
 def column(ext, y, shift=0):
-    return jnp.concatenate([ext[1 + x + shift, y : y + 1, :] for x in range(H)], axis=0)
+    return flat(ext)[strip(y, shift), :]
 
 
 def pack(sb, k, place, ext):
@@ -261,8 +269,7 @@
     if d[1] == 0:
         sb[k, place * B : (place + 1) * B, :] = ext[ex, MID, :]
     elif d[0] == 0:
-        for x in range(H):
-            sb[k, place * H + x : place * H + x + 1, :] = ext[1 + x, ey : ey + 1, :]
+        sb[k, place * H : (place + 1) * H, :] = column(ext, ey)
     else:
         sb[k, place : place + 1, :] = ext[ex, ey : ey + 1, :]
 
@@ -273,8 +280,7 @@
     if d[1] == 0:
         ext[hx, MID, :] = rb[k, place * B : (place + 1) * B, :]
     elif d[0] == 0:
-        for x in range(H):
-            ext[1 + x, hy : hy + 1, :] = rb[k, place * H + x : place * H + x + 1, :]
+        flat(ext)[strip(hy), :] = rb[k, place * H : (place + 1) * H, :]
     else:
         ext[hx, hy : hy + 1, :] = rb[k, place : place + 1, :]
 
@@ -330,15 +336,14 @@
         _, ey = edge_of((0, -dy))
         k = at[0, dy]
         n = places[k] * H
-        for x in range(H):
-            total = rb[k, n + x : n + x + 1, :]
-            for c in (-1, 0, 1):
-                total = total + q[SLOT[c, -dy], x + 1 - c, ey : ey + 1, :]
-            for dx in (-1, 1):
-                if x == (0 if dx > 0 else H - 1):
-                    kc = at[dx, dy]
-                    total = total + rb[kc, places[kc] + 1 : places[kc] + 2, :]
-            out[1 + x, hy : hy + 1, :] = total
+        total = rb[k, n : n + H, :]
+        for c in (-1, 0, 1):
+            total = total + column(q.at[SLOT[c, -dy]], ey, -c)
+        flat(out)[strip(hy), :] = total
+        for dx in (-1, 1):
+            kc = at[dx, dy]
+            ex, _ = edge_of((-dx, 0))
+            out[ex, hy : hy + 1, :] += rb[kc, places[kc] + 1 : places[kc] + 2, :]
     for dx in (-1, 1):
         for dy in (-1, 1):
             kc, kx, ky = at[dx, dy], at[dx, 0], at[0, dy]
@@ -365,8 +370,8 @@
 
 def kernel(
     nx, ny,
-    table, rates, pops_hbm, mask_hbm, class_hbm, cot_hbm, base_hbm, extra_hbm,
-    pops, cot, mask, wall_class, state, base_out, extra,
+    table_hbm, rates_hbm, pops_hbm, mask_hbm, class_hbm, cot_hbm, base_out, extra,
+    table, rates, pops, cot, mask, wall_class, state,
     psi_ext, solid_ext, wall_ext, e2_ext, sum_ext, d_ext, q_ext, cot_ext, post_ext, base_ext,
     s0, s1, s2, s3, s4, r0, r1, r2, r3, r4,
     send_sem, recv_sem, local_sem,
@@ -384,7 +389,7 @@
     loads = [
         pltpu.make_async_copy(src, dst, local_sem.at[n])
         for n, (src, dst) in enumerate(
-            ((pops_hbm, pops), (mask_hbm, mask), (class_hbm, wall_class), (cot_hbm, cot))
+            ((pops_hbm, pops), (mask_hbm, mask), (class_hbm, wall_class), (table_hbm, table), (rates_hbm, rates), (cot_hbm, cot))
         )
     ]
     for c in loads:
@@ -412,12 +417,11 @@
             body(x)
             return carry
 
-        lax.fori_loop(0, H, step, 0)
-
+        lax.fori_loop(0, H, step, 0, unroll=8)
+
+    for c in loads[:5]:
+        c.wait()
     rate = [rates[k] for k in range(19)]
-
-    for c in loads[:3]:
-        c.wait()
 
     def prepare(x):
         f = [pops[i, x] for i in range(19)]
@@ -440,7 +444,7 @@
     for k in range(8):
         pack(s0, k, 0, psi_ext)
 
-    loads[3].wait()
+    loads[5].wait()
 
     def turn(x):
         for i, c in enumerate(VELOCITY):
@@ -506,7 +510,11 @@
             if d[1] == 0:
                 where = [(hx, MID)]
             elif d[0] == 0:
-                where = [(1 + x, slice(hy, hy + 1)) for x in range(H)]
+                total = column(post_ext.at[MEMBERS[c][0]], hy)
+                for i in MEMBERS[c][1:]:
+                    total = total + column(post_ext.at[i], hy)
+                flat(q_ext.at[SLOT[c]])[strip(hy), :] = total
+                continue
             else:
                 where = [(hx, slice(hy, hy + 1))]
             for x, y in where:
@@ -528,7 +536,7 @@
         e2_ext[x] = jnp.where(solid, 0.0, fade)
         return carry
 
-    lax.fori_loop(0, H + 2, potential, 0)
+    lax.fori_loop(0, H + 2, potential, 0, unroll=10)
 
     def spread_out(fbar, psi, x):
         p = [5.0 * psi * v for v in fbar]
@@ -597,7 +605,7 @@
             d_ext[c + 1, x] = roll_z(v, -c)
         return carry
 
-    lax.fori_loop(0, H + 2, shift_second, 0)
+    lax.fori_loop(0, H + 2, shift_second, 0, unroll=10)
 
     def backward_first(x):
         solid = mask[x] == 1
@@ -623,8 +631,6 @@
         for n, c in enumerate(chosen_classes(d)):
             pack(s4, k, n, q_ext.at[SLOT[c]])
     last = start(4, 3)
-    store = pltpu.make_async_copy(base_out, base_hbm, local_sem.at[4])
-    store.start()
     finish(last)
     for k, d in enumerate(DIRS):
         for n, c in enumerate(chosen_classes(d)):
@@ -638,10 +644,22 @@
         extra[3, x] += jnp.where(mask[x] == 1, total, 0.0)
 
     each_row(spread_first)
-    rest = pltpu.make_async_copy(extra, extra_hbm, local_sem.at[5])
-    rest.start()
-    rest.wait()
-    store.wait()
+
+
+def closing(base, extra, adjoint_hbm, density_hbm, wet_hbm, adjoint, sems):
+    copies = [
+        pltpu.make_async_copy(extra.at[pl.ds(1, 2)], density_hbm, sems.at[19]),
+        pltpu.make_async_copy(extra.at[3], wet_hbm, sems.at[20]),
+    ]
+    for c in copies:
+        c.start()
+    for i in range(19):
+        adjoint[i] = base[i] + extra[0]
+        c = pltpu.make_async_copy(adjoint.at[i], adjoint_hbm.at[i], sems.at[i])
+        c.start()
+        copies.append(c)
+    for c in copies:
+        c.wait()
 
 
 def body(populations, solid_mask, wall_class, wall_table, relax_rates, pop_cotangent):
@@ -650,24 +668,27 @@
     block = (H, B, Z)
     ext = (H + 2, 32, Z)
     anywhere = pl.BlockSpec(memory_space=pl.ANY)
-    scalars = pl.BlockSpec(memory_space=pltpu.SMEM)
     vmem = pltpu.VMEM
+    far = [
+        pltpu.with_memory_space_constraint(v, pltpu.HBM)
+        for v in (wall_table, relax_rates, populations, solid_mask, wall_class, pop_cotangent)
+    ]
     base, extra = pl.pallas_call(
         functools.partial(kernel, nx, ny),
         out_shape=(
-            jax.ShapeDtypeStruct((19,) + block, f32),
-            jax.ShapeDtypeStruct((4,) + block, f32),
+            vmem((19,) + block, f32),
+            vmem((4,) + block, f32),
         ),
-        in_specs=[scalars, scalars] + [anywhere] * 4,
-        out_specs=(anywhere, anywhere),
+        in_specs=[anywhere] * 6,
+        out_specs=(pl.BlockSpec(memory_space=vmem),) * 2,
         scratch_shapes=[
+            pltpu.SMEM((8,), f32),
+            pltpu.SMEM((19,), f32),
             vmem((19,) + block, f32),
             vmem((19,) + block, f32),
             vmem(block, jnp.int32),
             vmem(block, jnp.int32),
             vmem((12,) + block, f32),
-            vmem((19,) + block, f32),
-            vmem((4,) + block, f32),
             vmem(ext, f32), vmem(ext, f32), vmem(ext, f32), vmem(ext, f32), vmem(ext, f32),
             vmem((3,) + ext, f32),
             vmem((9,) + ext, f32),
@@ -682,10 +703,21 @@
             pltpu.SemaphoreType.DMA((6,)),
         ],
         compiler_params=pltpu.CompilerParams(
-            collective_id=0, has_side_effects=True, vmem_limit_bytes=48 * 2**20
+            collective_id=0, has_side_effects=True, vmem_limit_bytes=40 * 2**20
         ),
-    )(wall_table, relax_rates, populations, solid_mask, wall_class, pop_cotangent)
-    return base + extra[0][None], extra[1:3], extra[3]
+    )(*far)
+    return pl.pallas_call(
+        closing,
+        out_shape=(
+            jax.ShapeDtypeStruct((19,) + block, f32),
+            jax.ShapeDtypeStruct((2,) + block, f32),
+            jax.ShapeDtypeStruct(block, f32),
+        ),
+        in_specs=[pl.BlockSpec(memory_space=vmem)] * 2,
+        out_specs=(anywhere,) * 3,
+        scratch_shapes=[vmem((19,) + block, f32), pltpu.SemaphoreType.DMA((21,))],
+        compiler_params=pltpu.CompilerParams(vmem_limit_bytes=8 * 2**20),
+    )(base, extra)
 
 
 def solution(mesh):

time: 44.8 us -> 34.5 us (0.77)
  local copies, waits for them, and re-layouts: 6.87 us -> 0 us
  Pallas kernels: 35.9 us -> 33.7 us
  other arithmetic: 1.15 us -> 0 us
    unnamed x12 -> x0, local copies, waits for them, and re-layouts: 5.57 us -> none
    pallas_call x1 -> x2, Pallas kernels: 35.9 us -> 33.7 us  [the longest x1 32.4 us: body(): pl.pallas_call(functools.partial(kernel, nx, ny), out_shape=(vmem((19,) +...]
    add x1 -> x0, other arithmetic: 1.15 us -> none  [body(): return (base + extra[0][None], extra[1:3], extra[3])]
    slice x1 -> x0, local copies, waits for them, and re-layouts: 0.66 us -> none  [body(): return (base + extra[0][None], extra[1:3], extra[3])]
    squeeze x1 -> x0, local copies, waits for them, and re-layouts: 0.64 us -> none  [body(): return (base + extra[0][None], extra[1:3], extra[3])]
where the time goes in v1:
time: 34.5 us; the launch traced here: 34.4 us
  Pallas kernels  33.7 us (98%)
  between operations  0.64 us (2%)
    pallas_call x1, Pallas kernels, body(): pl.pallas_call(functools.partial(kernel, nx, ny), out_shape=(vmem((19,) +...  32.4 us
    pallas_call x1, Pallas kernels, body(): pl.pallas_call(closing, out_shape=(jax.ShapeDtypeStruct((19,) + block, f3...  1.26 us

profile of v1, /device:TPU:0, one launch (start us, length us, event | category | flops | bytes accessed | tf_op | source)
XLA Modules:
  0.0 34.4 jit_solution(15338659052134310584)
XLA Ops:
  0.6 32.4 %shard_map.85 = (f32[19,8,16,128]{3,2,1,0:T(8,128)S(1)}, f32[4,8,16,128]{3,2,1,0:T(8,128)S(1)}) custom-call(f32[8]{0:T(128)} %table_hbm.1, f32[19]{0:T(128)} %rates_hbm.1, f32[19,8,16,128]{3,2,1,0:T(8,128)} %pops_hbm.1, s32[8,16,128]{2,1,0:T(8,128)} %mask_hbm.1, s32[8,16,128]{2,1,0:T(8,128)} %class_hbm.1, f32[19,8,16,128]{3,2,1,0:T(8,128)} %cot_hbm.1), custom_call_target="tpu_custom_call" | custom-call | tf_op jit(solution)/shard_map/pallas_call | solution.py:676
  33.1 1.3 %shard_map.86 = (f32[19,8,16,128]{3,2,1,0:T(8,128)}, f32[2,8,16,128]{3,2,1,0:T(8,128)}, f32[8,16,128]{2,1,0:T(8,128)}) custom-call(f32[19,8,16,128]{3,2,1,0:T(8,128)S(1)} %get-tuple-element.5.base, f32[4,8,16,128]{3,2,1,0:T(8,128)S(1)} %get-tuple-element.6.extra), custom_call_target="tpu_custom_call" | custom-call | tf_op jit(solution)/shard_map/pallas_call | solution.py:709

commit v2 on v1

v2 whole, which is shorter than its diff:
```python
import functools

import jax
import jax.numpy as jnp
from jax import lax
from jax.experimental import pallas as pl
from jax.experimental.pallas import tpu as pltpu
from jax.sharding import PartitionSpec as P

MESH = pl.DeviceIdType.MESH
VELOCITY = [
    (0, 0, 0),
    (1, 0, 0), (-1, 0, 0), (0, 1, 0), (0, -1, 0), (0, 0, 1), (0, 0, -1),
    (1, 1, 0), (-1, -1, 0), (1, -1, 0), (-1, 1, 0),
    (1, 0, 1), (-1, 0, -1), (1, 0, -1), (-1, 0, 1),
    (0, 1, 1), (0, -1, -1), (0, 1, -1), (0, -1, 1),
]
FACE_W, EDGE_W = 1.0 / 18.0, 1.0 / 36.0
AXES = (0, 1, 2)
PAIRS = ((0, 1), (0, 2), (1, 2))
CROSS = {(0, 1): 4, (0, 2): 5, (1, 2): 6}
QUAD = {(0, 1): 16, (0, 2): 17, (1, 2): 18}
CUBIC = {(0, 1): 10, (0, 2): 11, (1, 0): 12, (1, 2): 13, (2, 0): 14, (2, 1): 15}
EDGE = {(0, 1): 7, (0, 2): 11, (1, 2): 15}
ODD = (1, 2, 3, 10, 11, 12, 13, 14, 15)
OTHERS = {0: (1, 2), 1: (0, 2), 2: (0, 1)}
DIRS = ((-1, -1), (-1, 1), (1, -1), (1, 1), (-1, 0), (1, 0), (0, -1), (0, 1))
CLASSES = [(a, b) for a in (-1, 0, 1) for b in (-1, 0, 1)]
ACROSS, BESIDE = range(4), range(4, 8)
SLOT = {c: n for n, c in enumerate(CLASSES)}
MEMBERS = {c: [i for i, v in enumerate(VELOCITY) if v[:2] == c] for c in CLASSES}
H, B, Z = 8, 16, 128
Y0, Y1 = 8, 24
MID = slice(Y0, Y1)
ROWS = (16, 112, 104, 120, 16)


def quad(a, b):
    return QUAD[(min(a, b), max(a, b))]


def cross(a, b):
    return CROSS[(min(a, b), max(a, b))]


def roll_z(v, shift):
    return v if shift == 0 else pltpu.roll(v, shift % Z, v.ndim - 1)


def moments(f):
    m = [None] * 19
    s = [f[1 + 2 * a] + f[2 + 2 * a] for a in AXES]
    d = [f[1 + 2 * a] - f[2 + 2 * a] for a in AXES]
    for a, b in PAIRS:
        e = EDGE[a, b]
        al, ad = f[e] + f[e + 1], f[e] - f[e + 1]
        be, bd = f[e + 2] + f[e + 3], f[e + 2] - f[e + 3]
        m[CROSS[a, b]] = al - be
        m[QUAD[a, b]] = al + be
        m[CUBIC[a, b]] = ad + bd
        m[CUBIC[b, a]] = ad - bd
    for a in AXES:
        b, c = OTHERS[a]
        m[1 + a] = d[a] + (m[CUBIC[a, b]] + m[CUBIC[a, c]])
        m[7 + a] = s[a] + (m[quad(a, b)] + m[quad(a, c)])
    m[0] = (f[0] + s[0]) + (s[1] + s[2]) + (m[16] + m[17] + m[18])
    return m


def from_moments(p):
    f = [None] * 19
    for a in AXES:
        b, c = OTHERS[a]
        s = 0.5 * (p[7 + a] - (p[quad(a, b)] + p[quad(a, c)]))
        d = 0.5 * (p[1 + a] - (p[CUBIC[a, b]] + p[CUBIC[a, c]]))
        f[1 + 2 * a], f[2 + 2 * a] = s + d, s - d
    for a, b in PAIRS:
        e = EDGE[a, b]
        q, r = 0.25 * p[QUAD[a, b]], 0.25 * p[CROSS[a, b]]
        t, w = 0.25 * p[CUBIC[a, b]], 0.25 * p[CUBIC[b, a]]
        up, down, plus, minus = q + r, q - r, t + w, t - w
        f[e], f[e + 1], f[e + 2], f[e + 3] = up + plus, up - plus, down + minus, down - minus
    f[0] = p[0] - (p[7] + p[8] + p[9]) + (p[16] + p[17] + p[18])
    return f


def from_moments_t(lam):
    mu = [None] * 19
    mu[0] = lam[0]
    s = [0.5 * (lam[1 + 2 * a] + lam[2 + 2 * a]) for a in AXES]
    d = [0.5 * (lam[1 + 2 * a] - lam[2 + 2 * a]) for a in AXES]
    for a in AXES:
        mu[1 + a] = d[a]
        mu[7 + a] = s[a] - lam[0]
    for a, b in PAIRS:
        e = EDGE[a, b]
        al, ad = lam[e] + lam[e + 1], lam[e] - lam[e + 1]
        be, bd = lam[e + 2] + lam[e + 3], lam[e + 2] - lam[e + 3]
        mu[QUAD[a, b]] = 0.25 * (al + be) - s[a] - mu[7 + b]
        mu[CROSS[a, b]] = 0.25 * (al - be)
        mu[CUBIC[a, b]] = 0.25 * (ad + bd) - d[a]
        mu[CUBIC[b, a]] = 0.25 * (ad - bd) - d[b]
    return mu


def moments_t(nu):
    f = [None] * 19
    f[0] = nu[0]
    for a in AXES:
        s = nu[0] + nu[7 + a]
        f[1 + 2 * a], f[2 + 2 * a] = s + nu[1 + a], s - nu[1 + a]
    for a, b in PAIRS:
        e = EDGE[a, b]
        even = (nu[0] + nu[7 + a]) + (nu[7 + b] + nu[QUAD[a, b]])
        up, down = even + nu[CROSS[a, b]], even - nu[CROSS[a, b]]
        p, q = nu[1 + a] + nu[CUBIC[a, b]], nu[1 + b] + nu[CUBIC[b, a]]
        f[e], f[e + 1], f[e + 2], f[e + 3] = up + (p + q), up - (p + q), down + (p - q), down - (p - q)
    return f


def collide(f, psi, pull, inv, solid, rate):
    m = moments(f)
    rho = m[0]
    force = [5.0 * psi * g for g in pull]
    u = [(m[1 + a] + 0.5 * force[a]) * inv for a in AXES]
    n = [m[1 + a] - 0.5 * force[a] for a in AXES]
    p = [None] * 19
    p[0] = rho
    w = [u[a] * n[a] for a in AXES]
    t = [u[a] * force[a] for a in AXES]
    third = rho * (1.0 / 3.0)
    ninth = rho * (1.0 / 9.0)
    for a in AXES:
        p[1 + a] = m[1 + a] + force[a]
        k = 7 + a
        p[k] = m[k] + rate[k] * (third + w[a] - m[k]) + 2.0 * t[a]
    m3 = [m[1 + a] * (1.0 / 3.0) for a in AXES]
    f3 = [force[a] * (1.0 / 3.0) for a in AXES]
    for (a, b), k in CUBIC.items():
        p[k] = m[k] + rate[k] * (m3[a] - m[k]) + f3[a]
    w3 = [(1.0 / 3.0) * v for v in w]
    t3 = [(1.0 / 3.0) * v for v in t]
    for a, b in PAIRS:
        c = 3 - a - b
        k = CROSS[a, b]
        p[k] = m[k] + rate[k] * (0.5 * (u[b] * n[a] + u[a] * n[b]) - m[k]) + (u[a] * force[b] + u[b] * force[a])
        k = QUAD[a, b]
        p[k] = (
            m[k]
            + rate[k] * (ninth + (w3[a] + w3[b]) - 0.5 * w3[c] - m[k])
            + (2.0 * (t3[a] + t3[b]) - t3[c])
        )
    for k in range(1, 19):
        p[k] = jnp.where(solid, -m[k] if k in ODD else m[k], p[k])
    return from_moments(p), u, force


def adjoint_setup(lam, solid, rate):
    mu = from_moments_t(lam)
    e, nu, g = [None] * 19, [None] * 19, [None] * 19
    for k in (0,) + tuple(range(4, 19)):
        e[k] = rate[k] * mu[k]
        nu[k] = jnp.where(solid, -mu[k] if k in ODD else mu[k], mu[k] - e[k])
        g[k] = mu[k] - 0.5 * e[k]

    def diagonal(v):
        out = []
        for a in AXES:
            b, c = OTHERS[a]
            out.append(2.0 * v[7 + a] + (2.0 / 3.0) * (v[quad(a, b)] + v[quad(a, c)]) - (1.0 / 3.0) * v[quad(b, c)])
        return out

    def thirds(v):
        return [(1.0 / 3.0) * (v[CUBIC[a, OTHERS[a][0]]] + v[CUBIC[a, OTHERS[a][1]]]) for a in AXES]

    level = (
        e[0]
        + (1.0 / 3.0) * (e[7] + e[8] + e[9])
        + (1.0 / 9.0) * (e[16] + e[17] + e[18])
    )
    lift = [mu[1 + a] + v for a, v in enumerate(thirds(g))]
    return [nu[0]] + nu[4:] + mu[1:4] + diagonal(e) + e[4:7] + diagonal(g) + g[4:7] + thirds(e) + lift + [level]


SETUP = 38


def adjoint_finish(setup, u, force, inv, solid):
    nu = [setup[0], None, None, None] + list(setup[1:16])
    mu, ed, ec, gd, gc, push, lift = (setup[n : n + 3] for n in range(16, 37, 3))
    level = setup[37]

    def times(diag, off, x):
        out = []
        for a in AXES:
            b, c = OTHERS[a]
            out.append(diag[a] * x[a] + off[cross(a, b) - 4] * x[b] + off[cross(a, c) - 4] * x[c])
        return out

    eu, gu, gf = times(ed, ec, u), times(gd, gc, u), times(gd, gc, force)
    fbar = []
    for a in AXES:
        jbar = push[a] + eu[a] + gf[a] * inv
        nu[1 + a] = jnp.where(solid, -mu[a], mu[a] + jbar)
        fbar.append(jnp.where(solid, 0.0, lift[a] + gu[a] + 0.5 * jbar))
    rho_bar = (
        level
        - 0.5 * (u[0] * eu[0] + u[1] * eu[1] + u[2] * eu[2])
        - (force[0] * gu[0] + force[1] * gu[1] + force[2] * gu[2]) * inv
    )
    return nu, fbar, jnp.where(solid, 0.0, rho_bar)


class Row:
    def __init__(self, x):
        self.x = x

    def near(self, ext, a=0, b=0):
        return ext[self.x + 1 + a, Y0 + b : Y1 + b, :]

    def put(self, ext, v):
        ext[self.x + 1, MID, :] = v

    def own(self, ref):
        return ref[self.x]

    def keep(self, ref, v):
        ref[self.x] = v


class Column:
    def __init__(self, y):
        self.y = y

    def near(self, ext, a=0, b=0):
        return flat(ext)[strip(Y0 + self.y + b, a), :]

    def put(self, ext, v):
        flat(ext)[strip(Y0 + self.y), :] = v

    def own(self, ref):
        return ref.reshape(H * B, Z)[pl.ds(self.y, H, stride=B), :]

    def keep(self, ref, v):
        ref.reshape(H * B, Z)[pl.ds(self.y, H, stride=B), :] = v


def neighbour_pull(ext, part):
    at = {(a, b): part.near(ext, a, b) for a, b in CLASSES}
    dx, dy = at[1, 0] - at[-1, 0], at[0, 1] - at[0, -1]
    main, other = at[1, 1] - at[-1, -1], at[1, -1] - at[-1, 1]
    total = FACE_W * at[0, 0] + EDGE_W * ((at[1, 0] + at[-1, 0]) + (at[0, 1] + at[0, -1]))
    gx = FACE_W * dx + EDGE_W * (main + other + (roll_z(dx, 1) + roll_z(dx, -1)))
    gy = FACE_W * dy + EDGE_W * (main - other + (roll_z(dy, 1) + roll_z(dy, -1)))
    return [gx, gy, roll_z(total, -1) - roll_z(total, 1)]


def spread_classes(p):
    px, py, pz = p
    up, down = roll_z(pz, 1), roll_z(pz, -1)
    turned = [EDGE_W * (roll_z(v, 1) + roll_z(v, -1)) + FACE_W * v for v in (px, py)]
    lift = EDGE_W * (up - down)
    both, apart = EDGE_W * (px + py), EDGE_W * (px - py)
    return {
        (0, 0): FACE_W * (up - down),
        (1, 0): turned[0] + lift, (-1, 0): lift - turned[0],
        (0, 1): turned[1] + lift, (0, -1): lift - turned[1],
        (1, 1): both, (-1, -1): -both, (1, -1): apart, (-1, 1): -apart,
    }


def chosen(d, orient):
    return [i for i, v in enumerate(VELOCITY) if all(d[n] == 0 or v[n] == orient * d[n] for n in (0, 1))]


def edge_of(d):
    return (1 if d[0] < 0 else H), (Y0 if d[1] < 0 else Y1 - 1)


def halo_of(d):
    return (0 if d[0] < 0 else H + 1), (Y0 - 1 if d[1] < 0 else Y1)


def strip(y, shift=0):
    return pl.ds((1 + shift) * 32 + y, H, stride=32)


def flat(ext):
    return ext.reshape((H + 2) * 32, Z)


def pack(sb, k, place, ext):
    d = DIRS[k]
    ex, ey = edge_of(d)
    if d[1] == 0:
        sb[k, place * B : (place + 1) * B, :] = ext[ex, MID, :]
    elif d[0] == 0:
        sb[k, place * H : (place + 1) * H, :] = flat(ext)[strip(ey), :]
    else:
        sb[k, place : place + 1, :] = ext[ex, ey : ey + 1, :]


def unpack(rb, k, place, ext):
    d = DIRS[k]
    hx, hy = halo_of((-d[0], -d[1]))
    if d[1] == 0:
        ext[hx, MID, :] = rb[k, place * B : (place + 1) * B, :]
    elif d[0] == 0:
        flat(ext)[strip(hy), :] = rb[k, place * H : (place + 1) * H, :]
    else:
        ext[hx, hy : hy + 1, :] = rb[k, place : place + 1, :]


def shifted(v, step):
    rows = v.shape[0]
    index = lax.broadcasted_iota(jnp.int32, v.shape, 0)
    return jnp.where(index == (0 if step > 0 else rows - 1), 0.0, pltpu.roll(v, step % rows, 0))


def line(t):
    size = t[0].shape[0]
    return t[0] + shifted(t[1], 1) + shifted(t[-1], -1), t[-1][0:1, :], t[1][size - 1 : size, :]


def size_of(d):
    return B if d[1] == 0 else H


def lines_towards(q, d):
    ex, ey = edge_of(d)
    if d[1] == 0:
        outer = {c: q[SLOT[d[0], c], ex, MID, :] for c in (-1, 0, 1)}
        behind = {c: q[SLOT[0, c], ex, MID, :] + q[SLOT[d[0], c], ex - d[0], MID, :] for c in (-1, 0, 1)}
    else:
        def column(c, y):
            return flat(q.at[SLOT[c]])[strip(y), :]

        outer = {c: column((c, d[1]), ey) for c in (-1, 0, 1)}
        behind = {c: column((c, 0), ey) + column((c, d[1]), ey - d[1]) for c in (-1, 0, 1)}
    return line(outer), line(behind)


def put_lines(sb, k, fields, lines, ends=True):
    s = size_of(DIRS[k])
    at = fields * s
    for n, (middle, low, high) in enumerate(lines):
        sb[k, at + n * s : at + (n + 1) * s, :] = middle
        if ends:
            e = at + len(lines) * s + 2 * n
            sb[k, e : e + 1, :] = low
            sb[k, e + 1 : e + 2, :] = high


def get_lines(rb, k, fields, count, ends=True):
    s = size_of(DIRS[k])
    at = fields * s
    out = []
    for n in range(count):
        e = at + count * s + 2 * n
        low, high = (rb[k, e : e + 1, :], rb[k, e + 1 : e + 2, :]) if ends else (None, None)
        out.append((rb[k, at + n * s : at + (n + 1) * s, :], low, high))
    return out


def put_corner(sb, k, place, q):
    dx, dy = DIRS[k]
    ex, ey = edge_of((dx, dy))

    def one(c, x, y):
        return q[SLOT[c], x, y : y + 1, :]

    across = (dx, dy)
    values = (
        one((0, 0), ex, ey) + one((dx, 0), ex - dx, ey) + one((0, dy), ex, ey - dy) + one(across, ex - dx, ey - dy),
        one((dx, 0), ex, ey) + one(across, ex, ey - dy),
        one((0, dy), ex, ey) + one(across, ex - dx, ey),
        one(across, ex, ey),
    )
    for n, v in enumerate(values):
        sb[k, place + n : place + n + 1, :] = v


def own_sum(q, out, border=True):
    for x in range(0 if border else 1, H + 2 if border else H + 1):
        total = None
        for c in CLASSES:
            if 1 <= x - c[0] <= H:
                v = q[SLOT[c], x - c[0], Y0 - c[1] : Y1 - c[1], :]
                total = v if total is None else total + v
        out[x, MID, :] = total
    if not border:
        return
    for d in DIRS:
        ex, ey = edge_of(d)
        hx, hy = halo_of(d)
        if d[0] == 0:
            total = None
            for c in (-1, 0, 1):
                v = flat(q.at[SLOT[c, d[1]]])[strip(ey, -c), :]
                total = v if total is None else total + v
            flat(out)[strip(hy), :] = total
        elif d[1] != 0:
            out[hx, hy : hy + 1, :] = q[SLOT[d], ex, ey : ey + 1, :]


def add_line(out, d, at, middle, low, high):
    if d[1] == 0:
        out[at, MID, :] += middle
        if low is not None:
            out[at, Y0 - 1 : Y0, :] += low
            out[at, Y1 : Y1 + 1, :] += high
    else:
        flat(out)[strip(at), :] += middle
        if low is not None:
            out[0, at : at + 1, :] += low
            out[H + 1, at : at + 1, :] += high


def add_arrived(rb, out, k, into, behind, fields):
    d = DIRS[k]
    back = (-d[0], -d[1])
    ex, ey = edge_of(back)
    hx, hy = halo_of(back)
    if d[0] == 0 or d[1] == 0:
        n = 1 if d[0] == 0 else 0
        add_line(out, d, (ex, ey)[n], *into)
        if behind is not None:
            add_line(out, d, (hx, hy)[n], *behind)
    elif behind is None:
        out[ex, ey : ey + 1, :] += into
    else:
        for n, (x, y) in enumerate(((hx, hy), (ex, hy), (hx, ey), (ex, ey))):
            out[x, y : y + 1, :] += rb[k, fields + n : fields + n + 1, :]


def kernel(
    nx, ny,
    table_hbm, rates_hbm, pops_hbm, mask_hbm, class_hbm, cot_hbm, base_out, extra,
    table, rates, pops, cot, mask, wall_class, state, setup,
    psi_ext, solid_ext, wall_ext, e2_ext, sum_ext, d_ext, q_ext, cot_ext, post_ext, base_ext,
    s0, s1, s2, s3, s4, r0, r1, r2, r3, r4,
    send_sem, recv_sem, local_sem,
):
    gx, gy = lax.axis_index("gx"), lax.axis_index("gy")
    sends, recvs = (s0, s1, s2, s3, s4), (r0, r1, r2, r3, r4)

    def device(d):
        return (lax.rem(gx + (d[0] + nx), nx), lax.rem(gy + (d[1] + ny), ny))

    barrier = pltpu.get_barrier_semaphore()
    for d in DIRS:
        pl.semaphore_signal(barrier, inc=1, device_id=device(d), device_id_type=MESH)

    loads = [
        pltpu.make_async_copy(src, dst, local_sem.at[n])
        for n, (src, dst) in enumerate(
            ((pops_hbm, pops), (mask_hbm, mask), (class_hbm, wall_class), (table_hbm, table), (rates_hbm, rates), (cot_hbm, cot))
        )
    ]
    for c in loads:
        c.start()

    def start(r, fields, ends=0):
        copies = []
        for k, d in enumerate(DIRS):
            rows = pl.ds(0, fields * size_of(d) + ends if d[0] == 0 or d[1] == 0 else 8)
            c = pltpu.make_async_remote_copy(
                src_ref=sends[r].at[k, rows], dst_ref=recvs[r].at[k, rows],
                send_sem=send_sem.at[r, k], recv_sem=recv_sem.at[r, k],
                device_id=device(d), device_id_type=MESH,
            )
            c.start()
            copies.append(c)
        return copies

    def finish(copies, which=range(8)):
        for k in which:
            copies[k].wait()

    def each_row(body, first=0, last=H):
        def step(x, carry):
            body(Row(x))
            return carry

        lax.fori_loop(first, last, step, 0, unroll=last - first)

    def clear(x, carry):
        for n in range(9):
            q_ext[n, x] = jnp.zeros((32, Z), jnp.float32)
        return carry

    lax.fori_loop(0, H + 2, clear, 0)

    for c in loads[:5]:
        c.wait()
    rate = [rates[k] for k in range(19)]

    def prepare(part):
        f = [part.own(pops.at[i]) for i in range(19)]
        rho = f[0]
        for i in range(1, 19):
            rho = rho + f[i]
        solid = part.own(mask) == 1
        kind = part.own(wall_class)
        wall = jnp.full(rho.shape, table[0], jnp.float32)
        for n in range(1, 8):
            wall = jnp.where(kind == n, table[n], wall)
        fade = jnp.exp(-rho)
        part.put(psi_ext, jnp.where(solid, wall, 1.0 - fade))
        part.put(solid_ext, jnp.where(solid, 1.0, 0.0))
        part.put(wall_ext, wall)
        part.keep(state.at[0], 1.0 / rho)
        part.keep(state.at[11], jnp.where(solid, 0.0, fade))

    each_row(prepare)
    for k in range(8):
        pack(s0, k, 0, psi_ext)
    pl.semaphore_wait(barrier, len(DIRS))
    first = start(0, 1)

    loads[5].wait()

    def turn(part):
        for i, c in enumerate(VELOCITY):
            part.put(cot_ext.at[i], roll_z(part.own(cot.at[i]), -c[2]))

    each_row(turn)
    for k, d in enumerate(DIRS):
        ids = chosen(d, -1)
        for n, i in enumerate(ids):
            pack(s1, k, n, cot_ext.at[i])
        pack(s1, k, len(ids), solid_ext)
        pack(s1, k, len(ids) + 1, wall_ext)
    early = start(1, 7)

    def forward(part):
        psi = part.near(psi_ext)
        pull = neighbour_pull(psi_ext, part)
        f = [part.own(pops.at[i]) for i in range(19)]
        post, u, force = collide(f, psi, pull, part.own(state.at[0]), part.own(mask) == 1, rate)
        post = [roll_z(v, c[2]) for v, c in zip(post, VELOCITY)]
        for i in range(19):
            part.put(post_ext.at[i], post[i])
        for c in CLASSES:
            total = post[MEMBERS[c][0]]
            for i in MEMBERS[c][1:]:
                total = total + post[i]
            part.put(q_ext.at[SLOT[c]], total)
        for a in AXES:
            part.keep(state.at[1 + a], u[a])
            part.keep(state.at[4 + a], force[a])
            part.keep(state.at[7 + a], pull[a])
        part.keep(state.at[10], psi)

    each_row(forward, 1, H - 1)
    finish(first, BESIDE)
    for k in BESIDE:
        unpack(r0, k, 0, psi_ext)
    for part in (Column(0), Column(B - 1)):
        forward(part)
    finish(first, ACROSS)
    for k in ACROSS:
        unpack(r0, k, 0, psi_ext)
    for part in (Row(0), Row(H - 1)):
        forward(part)
    for k, d in enumerate(DIRS):
        ids = chosen(d, 1)
        for n, i in enumerate(ids):
            pack(s2, k, n, post_ext.at[i])
        if len(ids) == 1:
            put_corner(s2, k, 1, q_ext)
        else:
            put_lines(s2, k, 5, lines_towards(q_ext, d)[1:])
    second = start(2, 6, 8)

    own_sum(q_ext, sum_ext)
    finish(early)
    for k, d in enumerate(DIRS):
        ids = chosen(d, -1)
        for n, i in enumerate(ids):
            unpack(r1, k, n, cot_ext.at[i])
        unpack(r1, k, len(ids), solid_ext)
        unpack(r1, k, len(ids) + 1, wall_ext)

    def prepare_adjoint(part):
        lam = [part.near(cot_ext.at[i], c[0], c[1]) for i, c in enumerate(VELOCITY)]
        for n, v in enumerate(adjoint_setup(lam, part.own(mask) == 1, rate)):
            part.keep(setup.at[n], v)

    each_row(prepare_adjoint)
    finish(second, BESIDE)

    for k in BESIDE:
        d = DIRS[k]
        ids = chosen(d, 1)
        for n, i in enumerate(ids):
            unpack(r2, k, n, post_ext.at[i])
        s = size_of(d)
        parts = {}
        for n, i in enumerate(ids):
            c = VELOCITY[i][1 if d[1] == 0 else 0]
            v = r2[k, n * s : (n + 1) * s, :]
            parts[c] = parts[c] + v if c in parts else v
        add_arrived(r2, sum_ext, k, line(parts), get_lines(r2, k, 5, 1)[0], 5)

    def potential(x):
        solid = solid_ext[x] > 0.5
        fade = jnp.exp(-sum_ext[x])
        psi_ext[x] = jnp.where(solid, wall_ext[x], 1.0 - fade)
        e2_ext[x] = jnp.where(solid, 0.0, fade)

    for x in range(2, H):
        potential(x)

    def spread_out(fbar, psi, part):
        p = [5.0 * psi * v for v in fbar]
        for c, v in spread_classes(p).items():
            part.put(q_ext.at[SLOT[c]], v)

    def backward_second(part):
        inv = 1.0 / part.near(sum_ext)
        psi = part.near(psi_ext)
        solid = part.own(mask) == 1
        pull = neighbour_pull(psi_ext, part)
        force = [5.0 * psi * g for g in pull]
        f = [part.near(post_ext.at[i], -c[0], -c[1]) for i, c in enumerate(VELOCITY)]
        u = []
        for a in AXES:
            m = None
            for i, c in enumerate(VELOCITY):
                if c[a] == 1:
                    m = f[i] if m is None else m + f[i]
            for i, c in enumerate(VELOCITY):
                if c[a] == -1:
                    m = m - f[i]
            u.append((m + 0.5 * force[a]) * inv)
        ready = [part.own(setup.at[n]) for n in range(SETUP)]
        nu, fbar, rho_bar = adjoint_finish(ready, u, force, inv, solid)
        local = rho_bar + part.near(e2_ext) * (
            5.0 * (pull[0] * fbar[0] + pull[1] * fbar[1] + pull[2] * fbar[2])
        )
        part.keep(extra.at[2], local)
        nu[0] = nu[0] + local
        for i, v in enumerate(moments_t(nu)):
            part.put(base_ext.at[i], roll_z(v, -VELOCITY[i][2]))
        spread_out(fbar, psi, part)

    each_row(backward_second, 2, H - 2)
    finish(second, ACROSS)
    for k in ACROSS:
        unpack(r2, k, 0, post_ext.at[chosen(DIRS[k], 1)[0]])
        add_arrived(r2, sum_ext, k, True, True, 1)
    for x in (0, 1, H, H + 1):
        potential(x)
    for x in (0, 1, H - 2, H - 1):
        backward_second(Row(x))
    for k, d in enumerate(DIRS):
        ids = chosen(d, -1)
        for n, i in enumerate(ids):
            pack(s3, k, n, base_ext.at[i])
        if len(ids) == 1:
            put_corner(s3, k, 1, q_ext)
        else:
            put_lines(s3, k, 5, lines_towards(q_ext, d))
    third = start(3, 7, 8)
    own_sum(q_ext, sum_ext)
    finish(third, BESIDE)
    for k in BESIDE:
        for n, i in enumerate(chosen(DIRS[k], -1)):
            unpack(r3, k, n, base_ext.at[i])
        add_arrived(r3, sum_ext, k, *get_lines(r3, k, 5, 2), 5)

    def shift_second(x):
        v = e2_ext[x] * sum_ext[x]
        for c in (-1, 0, 1):
            d_ext[c + 1, x] = roll_z(v, -c)

    for x in range(2, H):
        shift_second(x)
    finish(third, ACROSS)
    for k in ACROSS:
        unpack(r3, k, 0, base_ext.at[chosen(DIRS[k], -1)[0]])
        add_arrived(r3, sum_ext, k, True, True, 1)
    for x in (0, 1, H, H + 1):
        shift_second(x)

    def backward_first(part):
        solid = part.own(mask) == 1
        inv, psi = part.own(state.at[0]), part.own(state.at[10])
        u = [part.own(state.at[1 + a]) for a in AXES]
        force = [part.own(state.at[4 + a]) for a in AXES]
        lam = [
            part.near(base_ext.at[i], c[0], c[1]) + part.near(d_ext.at[c[2] + 1], c[0], c[1])
            for i, c in enumerate(VELOCITY)
        ]
        nu, fbar, rho_bar = adjoint_finish(adjoint_setup(lam, solid, rate), u, force, inv, solid)
        spread_out(fbar, psi, part)
        if isinstance(part, Column):
            return
        pull = [part.own(state.at[7 + a]) for a in AXES]
        local = rho_bar + part.own(state.at[11]) * (
            5.0 * (pull[0] * fbar[0] + pull[1] * fbar[1] + pull[2] * fbar[2])
        )
        part.keep(extra.at[1], local)
        nu[0] = nu[0] + local
        for i, v in enumerate(moments_t(nu)):
            part.keep(base_out.at[i], v)

    for part in (Row(0), Row(H - 1), Column(0), Column(B - 1)):
        backward_first(part)
    for k, d in enumerate(DIRS):
        if d[0] == 0 or d[1] == 0:
            put_lines(s4, k, 0, lines_towards(q_ext, d)[:1], False)
        else:
            pack(s4, k, 0, q_ext.at[SLOT[d]])
    last = start(4, 1)

    def spread_second(part):
        total = part.near(sum_ext)
        part.keep(extra.at[2], part.own(extra.at[2]) + part.near(d_ext.at[1]))
        part.keep(extra.at[3], jnp.where(part.own(mask) == 1, total, 0.0))

    each_row(spread_second)
    each_row(backward_first, 1, H - 1)
    own_sum(q_ext, sum_ext, False)
    finish(last, BESIDE)
    for k in BESIDE:
        add_arrived(r4, sum_ext, k, get_lines(r4, k, 0, 1, False)[0], None, 0)

    def spread_first(part):
        total = part.near(sum_ext)
        change = part.own(state.at[11]) * total
        part.keep(extra.at[0], change)
        part.keep(extra.at[1], part.own(extra.at[1]) + change)
        part.keep(extra.at[3], part.own(extra.at[3]) + jnp.where(part.own(mask) == 1, total, 0.0))

    each_row(spread_first, 1, H - 1)
    finish(last, ACROSS)
    for k in ACROSS:
        add_arrived(r4, sum_ext, k, r4[k, 0:1, :], None, 0)
    for x in (0, H - 1):
        spread_first(Row(x))


def closing(base, extra, adjoint_hbm, density_hbm, wet_hbm, adjoint, sems):
    copies = [
        pltpu.make_async_copy(extra.at[pl.ds(1, 2)], density_hbm, sems.at[19]),
        pltpu.make_async_copy(extra.at[3], wet_hbm, sems.at[20]),
    ]
    for c in copies:
        c.start()
    for i in range(19):
        adjoint[i] = base[i] + extra[0]
        c = pltpu.make_async_copy(adjoint.at[i], adjoint_hbm.at[i], sems.at[i])
        c.start()
        copies.append(c)
    for c in copies:
        c.wait()


def body(populations, solid_mask, wall_class, wall_table, relax_rates, pop_cotangent):
    f32 = jnp.float32
    nx, ny = lax.axis_size("gx"), lax.axis_size("gy")
    block = (H, B, Z)
    ext = (H + 2, 32, Z)
    anywhere = pl.BlockSpec(memory_space=pl.ANY)
    vmem = pltpu.VMEM
    far = [
        pltpu.with_memory_space_constraint(v, pltpu.HBM)
        for v in (wall_table, relax_rates, populations, solid_mask, wall_class, pop_cotangent)
    ]
    base, extra = pl.pallas_call(
        functools.partial(kernel, nx, ny),
        out_shape=(
            vmem((19,) + block, f32),
            vmem((4,) + block, f32),
        ),
        in_specs=[anywhere] * 6,
        out_specs=(pl.BlockSpec(memory_space=vmem),) * 2,
        scratch_shapes=[
            pltpu.SMEM((8,), f32),
            pltpu.SMEM((19,), f32),
            vmem((19,) + block, f32),
            vmem((19,) + block, f32),
            vmem(block, jnp.int32),
            vmem(block, jnp.int32),
            vmem((12,) + block, f32),
            vmem((SETUP,) + block, f32),
            vmem(ext, f32), vmem(ext, f32), vmem(ext, f32), vmem(ext, f32), vmem(ext, f32),
            vmem((3,) + ext, f32),
            vmem((9,) + ext, f32),
            vmem((19,) + ext, f32),
            vmem((19,) + ext, f32),
            vmem((19,) + ext, f32),
        ]
        + [vmem((8, n, Z), f32) for n in ROWS] * 2
        + [
            pltpu.SemaphoreType.DMA((5, 8)),
            pltpu.SemaphoreType.DMA((5, 8)),
            pltpu.SemaphoreType.DMA((6,)),
        ],
        compiler_params=pltpu.CompilerParams(
            collective_id=0, has_side_effects=True, vmem_limit_bytes=40 * 2**20
        ),
    )(*far)
    return pl.pallas_call(
        closing,
        out_shape=(
            jax.ShapeDtypeStruct((19,) + block, f32),
            jax.ShapeDtypeStruct((2,) + block, f32),
            jax.ShapeDtypeStruct(block, f32),
        ),
        in_specs=[pl.BlockSpec(memory_space=vmem)] * 2,
        out_specs=(anywhere,) * 3,
        scratch_shapes=[vmem((19,) + block, f32), pltpu.SemaphoreType.DMA((21,))],
        compiler_params=pltpu.CompilerParams(vmem_limit_bytes=8 * 2**20),
    )(base, extra)


def solution(mesh):
    in_specs = (
        P(None, "gx", "gy", None),
        P("gx", "gy", None),
        P("gx", "gy", None),
        P(),
        P(),
        P(None, "gx", "gy", None),
    )
    out_specs = (P(None, "gx", "gy", None), P(None, "gx", "gy", None), P("gx", "gy", None))
    return jax.shard_map(body, mesh=mesh, in_specs=in_specs, out_specs=out_specs, check_vma=False)
```

time: 34.5 us -> 32.4 us (0.939)
  Pallas kernels: 33.7 us -> 31.6 us
    pallas_call x1, Pallas kernels: 32.4 us -> 30.4 us  [body(): pl.pallas_call(functools.partial(kernel, nx, ny), out_shape=(vmem((19,) +...]
where the time goes in v2:
time: 32.4 us; the launch traced here: 32.3 us
  Pallas kernels  31.6 us (98%)
  between operations  0.64 us (2%)
    pallas_call x1, Pallas kernels, body(): pl.pallas_call(functools.partial(kernel, nx, ny), out_shape=(vmem((19,) +...  30.4 us
    pallas_call x1, Pallas kernels, body(): pl.pallas_call(closing, out_shape=(jax.ShapeDtypeStruct((19,) + block, f3...  1.26 us

profile of v2, /device:TPU:0, one launch (start us, length us, event | category | flops | bytes accessed | tf_op | source)
XLA Modules:
  0.0 32.3 jit_solution(14104321323821284738)
XLA Ops:
  0.6 30.4 %shard_map.85 = (f32[19,8,16,128]{3,2,1,0:T(8,128)S(1)}, f32[4,8,16,128]{3,2,1,0:T(8,128)S(1)}) custom-call(f32[8]{0:T(128)} %table_hbm.1, f32[19]{0:T(128)} %rates_hbm.1, f32[19,8,16,128]{3,2,1,0:T(8,128)} %pops_hbm.1, s32[8,16,128]{2,1,0:T(8,128)} %mask_hbm.1, s32[8,16,128]{2,1,0:T(8,128)} %class_hbm.1, f32[19,8,16,128]{3,2,1,0:T(8,128)} %cot_hbm.1), custom_call_target="tpu_custom_call" | custom-call | tf_op jit(solution)/shard_map/pallas_call | solution.py:772
  31.0 1.3 %shard_map.86 = (f32[19,8,16,128]{3,2,1,0:T(8,128)}, f32[2,8,16,128]{3,2,1,0:T(8,128)}, f32[8,16,128]{2,1,0:T(8,128)}) custom-call(f32[19,8,16,128]{3,2,1,0:T(8,128)S(1)} %get-tuple-element.5.base, f32[4,8,16,128]{3,2,1,0:T(8,128)S(1)} %get-tuple-element.6.extra), custom_call_target="tpu_custom_call" | custom-call | tf_op jit(solution)/shard_map/pallas_call | solution.py:806

commit v3 on v2

--- a/solution.py
+++ b/solution.py
@@ -18,18 +18,20 @@
 FACE_W, EDGE_W = 1.0 / 18.0, 1.0 / 36.0
 AXES = (0, 1, 2)
 PAIRS = ((0, 1), (0, 2), (1, 2))
+H, B, Z = 8, 16, 128
 CROSS = {(0, 1): 4, (0, 2): 5, (1, 2): 6}
 QUAD = {(0, 1): 16, (0, 2): 17, (1, 2): 18}
 CUBIC = {(0, 1): 10, (0, 2): 11, (1, 0): 12, (1, 2): 13, (2, 0): 14, (2, 1): 15}
 EDGE = {(0, 1): 7, (0, 2): 11, (1, 2): 15}
 ODD = (1, 2, 3, 10, 11, 12, 13, 14, 15)
 OTHERS = {0: (1, 2), 1: (0, 2), 2: (0, 1)}
-DIRS = ((-1, -1), (-1, 1), (1, -1), (1, 1), (-1, 0), (1, 0), (0, -1), (0, 1))
+DIRS = ((-1, -1), (1, 1), (-1, 1), (1, -1), (-1, 0), (1, 0), (0, -1), (0, 1))
 CLASSES = [(a, b) for a in (-1, 0, 1) for b in (-1, 0, 1)]
 ACROSS, BESIDE = range(4), range(4, 8)
+PAIR_A, PAIR_B = range(2), range(2, 4)
+ENDS_A, ENDS_B = ((0, 0), (H - 1, B // 2)), ((0, B // 2), (H - 1, 0))
 SLOT = {c: n for n, c in enumerate(CLASSES)}
 MEMBERS = {c: [i for i, v in enumerate(VELOCITY) if v[:2] == c] for c in CLASSES}
-H, B, Z = 8, 16, 128
 Y0, Y1 = 8, 24
 MID = slice(Y0, Y1)
 ROWS = (16, 112, 104, 120, 16)
@@ -212,20 +214,22 @@
 
 
 class Row:
-    def __init__(self, x):
-        self.x = x
+    def __init__(self, x, first=0, count=B):
+        self.x, self.first, self.count = x, first, count
 
     def near(self, ext, a=0, b=0):
-        return ext[self.x + 1 + a, Y0 + b : Y1 + b, :]
+        y = Y0 + self.first + b
+        return ext[self.x + 1 + a, y : y + self.count, :]
 
     def put(self, ext, v):
-        ext[self.x + 1, MID, :] = v
+        y = Y0 + self.first
+        ext[self.x + 1, y : y + self.count, :] = v
 
     def own(self, ref):
-        return ref[self.x]
+        return ref[self.x, self.first : self.first + self.count, :]
 
     def keep(self, ref, v):
-        ref[self.x] = v
+        ref[self.x, self.first : self.first + self.count, :] = v
 
 
 class Column:
@@ -435,7 +439,7 @@
 
 def kernel(
     nx, ny,
-    table_hbm, rates_hbm, pops_hbm, mask_hbm, class_hbm, cot_hbm, base_out, extra,
+    table_hbm, rates_hbm, pops_hbm, mask_hbm, class_hbm, cot_hbm, base_out, density_out, wet_out,
     table, rates, pops, cot, mask, wall_class, state, setup,
     psi_ext, solid_ext, wall_ext, e2_ext, sum_ext, d_ext, q_ext, cot_ext, post_ext, base_ext,
     s0, s1, s2, s3, s4, r0, r1, r2, r3, r4,
@@ -460,9 +464,10 @@
     for c in loads:
         c.start()
 
-    def start(r, fields, ends=0):
-        copies = []
-        for k, d in enumerate(DIRS):
+    def start(r, fields, ends=0, which=range(8)):
+        copies = {}
+        for k in which:
+            d = DIRS[k]
             rows = pl.ds(0, fields * size_of(d) + ends if d[0] == 0 or d[1] == 0 else 8)
             c = pltpu.make_async_remote_copy(
                 src_ref=sends[r].at[k, rows], dst_ref=recvs[r].at[k, rows],
@@ -470,7 +475,7 @@
                 device_id=device(d), device_id_type=MESH,
             )
             c.start()
-            copies.append(c)
+            copies[k] = c
         return copies
 
     def finish(copies, which=range(8)):
@@ -561,17 +566,20 @@
     finish(first, ACROSS)
     for k in ACROSS:
         unpack(r0, k, 0, psi_ext)
-    for part in (Row(0), Row(H - 1)):
-        forward(part)
-    for k, d in enumerate(DIRS):
-        ids = chosen(d, 1)
-        for n, i in enumerate(ids):
+    second = {}
+    for pair, ends in ((PAIR_A, ENDS_A), (PAIR_B, ENDS_B)):
+        for x, y in ends:
+            forward(Row(x, y, B // 2))
+        for k in pair:
+            pack(s2, k, 0, post_ext.at[chosen(DIRS[k], 1)[0]])
+            put_corner(s2, k, 1, q_ext)
+        second.update(start(2, 6, 8, pair))
+    for k in BESIDE:
+        d = DIRS[k]
+        for n, i in enumerate(chosen(d, 1)):
             pack(s2, k, n, post_ext.at[i])
-        if len(ids) == 1:
-            put_corner(s2, k, 1, q_ext)
-        else:
-            put_lines(s2, k, 5, lines_towards(q_ext, d)[1:])
-    second = start(2, 6, 8)
+        put_lines(s2, k, 5, lines_towards(q_ext, d)[1:])
+    second.update(start(2, 6, 8, BESIDE))
 
     own_sum(q_ext, sum_ext)
     finish(early)
@@ -639,7 +647,7 @@
         local = rho_bar + part.near(e2_ext) * (
             5.0 * (pull[0] * fbar[0] + pull[1] * fbar[1] + pull[2] * fbar[2])
         )
-        part.keep(extra.at[2], local)
+        part.keep(density_out.at[1], local)
         nu[0] = nu[0] + local
         for i, v in enumerate(moments_t(nu)):
             part.put(base_ext.at[i], roll_z(v, -VELOCITY[i][2]))
@@ -652,17 +660,21 @@
         add_arrived(r2, sum_ext, k, True, True, 1)
     for x in (0, 1, H, H + 1):
         potential(x)
-    for x in (0, 1, H - 2, H - 1):
-        backward_second(Row(x))
-    for k, d in enumerate(DIRS):
-        ids = chosen(d, -1)
-        for n, i in enumerate(ids):
+    third = {}
+    for pair, ends in ((PAIR_A, ENDS_A), (PAIR_B, ENDS_B)):
+        for x, y in ends:
+            backward_second(Row(x, y, B // 2))
+            backward_second(Row(1 if x == 0 else H - 2, y, B // 2))
+        for k in pair:
+            pack(s3, k, 0, base_ext.at[chosen(DIRS[k], -1)[0]])
+            put_corner(s3, k, 1, q_ext)
+        third.update(start(3, 7, 8, pair))
+    for k in BESIDE:
+        d = DIRS[k]
+        for n, i in enumerate(chosen(d, -1)):
             pack(s3, k, n, base_ext.at[i])
-        if len(ids) == 1:
-            put_corner(s3, k, 1, q_ext)
-        else:
-            put_lines(s3, k, 5, lines_towards(q_ext, d))
-    third = start(3, 7, 8)
+        put_lines(s3, k, 5, lines_towards(q_ext, d))
+    third.update(start(3, 7, 8, BESIDE))
     own_sum(q_ext, sum_ext)
     finish(third, BESIDE)
     for k in BESIDE:
@@ -701,24 +713,28 @@
         local = rho_bar + part.own(state.at[11]) * (
             5.0 * (pull[0] * fbar[0] + pull[1] * fbar[1] + pull[2] * fbar[2])
         )
-        part.keep(extra.at[1], local)
+        part.keep(density_out.at[0], local)
         nu[0] = nu[0] + local
         for i, v in enumerate(moments_t(nu)):
             part.keep(base_out.at[i], v)
 
-    for part in (Row(0), Row(H - 1), Column(0), Column(B - 1)):
-        backward_first(part)
-    for k, d in enumerate(DIRS):
-        if d[0] == 0 or d[1] == 0:
-            put_lines(s4, k, 0, lines_towards(q_ext, d)[:1], False)
-        else:
-            pack(s4, k, 0, q_ext.at[SLOT[d]])
-    last = start(4, 1)
+    last = {}
+    for pair, ends in ((PAIR_A, ENDS_A), (PAIR_B, ENDS_B)):
+        for x, y in ends:
+            backward_first(Row(x, y, B // 2))
+        for k in pair:
+            pack(s4, k, 0, q_ext.at[SLOT[DIRS[k]]])
+        last.update(start(4, 1, 0, pair))
+    for y in (0, B - 1):
+        backward_first(Column(y))
+    for k in BESIDE:
+        put_lines(s4, k, 0, lines_towards(q_ext, DIRS[k])[:1], False)
+    last.update(start(4, 1, 0, BESIDE))
 
     def spread_second(part):
         total = part.near(sum_ext)
-        part.keep(extra.at[2], part.own(extra.at[2]) + part.near(d_ext.at[1]))
-        part.keep(extra.at[3], jnp.where(part.own(mask) == 1, total, 0.0))
+        part.keep(density_out.at[1], part.own(density_out.at[1]) + part.near(d_ext.at[1]))
+        part.keep(wet_out, jnp.where(part.own(mask) == 1, total, 0.0))
 
     each_row(spread_second)
     each_row(backward_first, 1, H - 1)
@@ -730,9 +746,10 @@
     def spread_first(part):
         total = part.near(sum_ext)
         change = part.own(state.at[11]) * total
-        part.keep(extra.at[0], change)
-        part.keep(extra.at[1], part.own(extra.at[1]) + change)
-        part.keep(extra.at[3], part.own(extra.at[3]) + jnp.where(part.own(mask) == 1, total, 0.0))
+        part.keep(density_out.at[0], part.own(density_out.at[0]) + change)
+        part.keep(wet_out, part.own(wet_out) + jnp.where(part.own(mask) == 1, total, 0.0))
+        for i in range(19):
+            part.keep(base_out.at[i], part.own(base_out.at[i]) + change)
 
     each_row(spread_first, 1, H - 1)
     finish(last, ACROSS)
@@ -742,18 +759,15 @@
         spread_first(Row(x))
 
 
-def closing(base, extra, adjoint_hbm, density_hbm, wet_hbm, adjoint, sems):
+def closing(adjoint, density, wet, adjoint_hbm, density_hbm, wet_hbm, sems):
     copies = [
-        pltpu.make_async_copy(extra.at[pl.ds(1, 2)], density_hbm, sems.at[19]),
-        pltpu.make_async_copy(extra.at[3], wet_hbm, sems.at[20]),
+        pltpu.make_async_copy(adjoint.at[pl.ds(n, 4 if n < 16 else 3)], adjoint_hbm.at[pl.ds(n, 4 if n < 16 else 3)], sems.at[n // 4])
+        for n in range(0, 19, 4)
     ]
+    copies.append(pltpu.make_async_copy(density, density_hbm, sems.at[10]))
+    copies.append(pltpu.make_async_copy(wet, wet_hbm, sems.at[11]))
     for c in copies:
         c.start()
-    for i in range(19):
-        adjoint[i] = base[i] + extra[0]
-        c = pltpu.make_async_copy(adjoint.at[i], adjoint_hbm.at[i], sems.at[i])
-        c.start()
-        copies.append(c)
     for c in copies:
         c.wait()
 
@@ -769,14 +783,15 @@
         pltpu.with_memory_space_constraint(v, pltpu.HBM)
         for v in (wall_table, relax_rates, populations, solid_mask, wall_class, pop_cotangent)
     ]
-    base, extra = pl.pallas_call(
+    results = pl.pallas_call(
         functools.partial(kernel, nx, ny),
         out_shape=(
             vmem((19,) + block, f32),
-            vmem((4,) + block, f32),
+            vmem((2,) + block, f32),
+            vmem(block, f32),
         ),
         in_specs=[anywhere] * 6,
-        out_specs=(pl.BlockSpec(memory_space=vmem),) * 2,
+        out_specs=(pl.BlockSpec(memory_space=vmem),) * 3,
         scratch_shapes=[
             pltpu.SMEM((8,), f32),
             pltpu.SMEM((19,), f32),
@@ -805,16 +820,12 @@
     )(*far)
     return pl.pallas_call(
         closing,
-        out_shape=(
-            jax.ShapeDtypeStruct((19,) + block, f32),
-            jax.ShapeDtypeStruct((2,) + block, f32),
-            jax.ShapeDtypeStruct(block, f32),
-        ),
-        in_specs=[pl.BlockSpec(memory_space=vmem)] * 2,
+        out_shape=tuple(jax.ShapeDtypeStruct(v.shape, f32) for v in results),
+        in_specs=[pl.BlockSpec(memory_space=vmem)] * 3,
         out_specs=(anywhere,) * 3,
-        scratch_shapes=[vmem((19,) + block, f32), pltpu.SemaphoreType.DMA((21,))],
+        scratch_shapes=[pltpu.SemaphoreType.DMA((12,))],
         compiler_params=pltpu.CompilerParams(vmem_limit_bytes=8 * 2**20),
-    )(base, extra)
+    )(*results)
 
 
 def solution(mesh):

time: 32.4 us -> 32.2 us (level)
  no operation moved by 1% of the time
where the time goes in v3:
time: 32.2 us; the launch traced here: 32 us
  Pallas kernels  31.4 us (98%)
  between operations  0.64 us (2%)
    pallas_call x1, Pallas kernels, body(): pl.pallas_call(functools.partial(kernel, nx, ny), out_shape=(vmem((19,) +...  30.2 us
    pallas_call x1, Pallas kernels, body(): pl.pallas_call(closing, out_shape=tuple((jax.ShapeDtypeStruct(v.shape, f3...  1.19 us

profile of v3, /device:TPU:0, one launch (start us, length us, event | category | flops | bytes accessed | tf_op | source)
XLA Modules:
  0.0 32.0 jit_solution(7967162119928464628)
XLA Ops:
  0.6 30.2 %shard_map.85 = (f32[19,8,16,128]{3,2,1,0:T(8,128)S(1)}, f32[2,8,16,128]{3,2,1,0:T(8,128)S(1)}, f32[8,16,128]{2,1,0:T(8,128)S(1)}) custom-call(f32[8]{0:T(128)} %table_hbm.1, f32[19]{0:T(128)} %rates_hbm.1, f32[19,8,16,128]{3,2,1,0:T(8,128)} %pops_hbm.1, s32[8,16,128]{2,1,0:T(8,128)} %mask_hbm.1, s32[8,16,128]{2,1,0:T(8,128)} %class_hbm.1, ...), custom_call_target="tpu_custom_call" | custom-call | tf_op jit(solution)/shard_map/pallas_call | solution.py:786
  30.8 1.2 %shard_map.86 = (f32[19,8,16,128]{3,2,1,0:T(8,128)}, f32[2,8,16,128]{3,2,1,0:T(8,128)}, f32[8,16,128]{2,1,0:T(8,128)}) custom-call(f32[19,8,16,128]{3,2,1,0:T(8,128)S(1)} %get-tuple-element.6.adjoint, f32[2,8,16,128]{3,2,1,0:T(8,128)S(1)} %get-tuple-element.7.density, f32[8,16,128]{2,1,0:T(8,128)S(1)} %get-tuple-element.8.wet), custom_call_target="tpu_custom_call" | custom-call | tf_op jit(solution)/shard_map/pallas_call | solution.py:821

commit v4 on v3

--- a/solution.py
+++ b/solution.py
@@ -32,6 +32,7 @@
 ENDS_A, ENDS_B = ((0, 0), (H - 1, B // 2)), ((0, B // 2), (H - 1, 0))
 SLOT = {c: n for n, c in enumerate(CLASSES)}
 MEMBERS = {c: [i for i, v in enumerate(VELOCITY) if v[:2] == c] for c in CLASSES}
+WIDE, TALL = 40, 24
 Y0, Y1 = 8, 24
 MID = slice(Y0, Y1)
 ROWS = (16, 112, 104, 120, 16)
@@ -243,10 +244,10 @@
         flat(ext)[strip(Y0 + self.y), :] = v
 
     def own(self, ref):
-        return ref.reshape(H * B, Z)[pl.ds(self.y, H, stride=B), :]
+        return ref.reshape(H * TALL, Z)[pl.ds(self.y, H, stride=TALL), :]
 
     def keep(self, ref, v):
-        ref.reshape(H * B, Z)[pl.ds(self.y, H, stride=B), :] = v
+        ref.reshape(H * TALL, Z)[pl.ds(self.y, H, stride=TALL), :] = v
 
 
 def neighbour_pull(ext, part):
@@ -286,11 +287,11 @@
 
 
 def strip(y, shift=0):
-    return pl.ds((1 + shift) * 32 + y, H, stride=32)
+    return pl.ds((1 + shift) * WIDE + y, H, stride=WIDE)
 
 
 def flat(ext):
-    return ext.reshape((H + 2) * 32, Z)
+    return ext.reshape((H + 2) * WIDE, Z)
 
 
 def pack(sb, k, place, ext):
@@ -458,7 +459,7 @@
     loads = [
         pltpu.make_async_copy(src, dst, local_sem.at[n])
         for n, (src, dst) in enumerate(
-            ((pops_hbm, pops), (mask_hbm, mask), (class_hbm, wall_class), (table_hbm, table), (rates_hbm, rates), (cot_hbm, cot))
+            ((pops_hbm, pops.at[:, :, pl.ds(0, B)]), (mask_hbm, mask.at[:, pl.ds(0, B)]), (class_hbm, wall_class), (table_hbm, table), (rates_hbm, rates), (cot_hbm, cot))
         )
     ]
     for c in loads:
@@ -491,7 +492,7 @@
 
     def clear(x, carry):
         for n in range(9):
-            q_ext[n, x] = jnp.zeros((32, Z), jnp.float32)
+            q_ext[n, x] = jnp.zeros((WIDE, Z), jnp.float32)
         return carry
 
     lax.fori_loop(0, H + 2, clear, 0)
@@ -611,11 +612,13 @@
             parts[c] = parts[c] + v if c in parts else v
         add_arrived(r2, sum_ext, k, line(parts), get_lines(r2, k, 5, 1)[0], 5)
 
+    used = slice(0, 32)
+
     def potential(x):
-        solid = solid_ext[x] > 0.5
-        fade = jnp.exp(-sum_ext[x])
-        psi_ext[x] = jnp.where(solid, wall_ext[x], 1.0 - fade)
-        e2_ext[x] = jnp.where(solid, 0.0, fade)
+        solid = solid_ext[x, used, :] > 0.5
+        fade = jnp.exp(-sum_ext[x, used, :])
+        psi_ext[x, used, :] = jnp.where(solid, wall_ext[x, used, :], 1.0 - fade)
+        e2_ext[x, used, :] = jnp.where(solid, 0.0, fade)
 
     for x in range(2, H):
         potential(x)
@@ -683,9 +686,9 @@
         add_arrived(r3, sum_ext, k, *get_lines(r3, k, 5, 2), 5)
 
     def shift_second(x):
-        v = e2_ext[x] * sum_ext[x]
+        v = e2_ext[x, used, :] * sum_ext[x, used, :]
         for c in (-1, 0, 1):
-            d_ext[c + 1, x] = roll_z(v, -c)
+            d_ext[c + 1, x, used, :] = roll_z(v, -c)
 
     for x in range(2, H):
         shift_second(x)
@@ -776,7 +779,7 @@
     f32 = jnp.float32
     nx, ny = lax.axis_size("gx"), lax.axis_size("gy")
     block = (H, B, Z)
-    ext = (H + 2, 32, Z)
+    ext = (H + 2, WIDE, Z)
     anywhere = pl.BlockSpec(memory_space=pl.ANY)
     vmem = pltpu.VMEM
     far = [
@@ -795,11 +798,11 @@
         scratch_shapes=[
             pltpu.SMEM((8,), f32),
             pltpu.SMEM((19,), f32),
+            vmem((19, H, TALL, Z), f32),
             vmem((19,) + block, f32),
-            vmem((19,) + block, f32),
+            vmem((H, TALL, Z), jnp.int32),
             vmem(block, jnp.int32),
-            vmem(block, jnp.int32),
-            vmem((12,) + block, f32),
+            vmem((12, H, TALL, Z), f32),
             vmem((SETUP,) + block, f32),
             vmem(ext, f32), vmem(ext, f32), vmem(ext, f32), vmem(ext, f32), vmem(ext, f32),
             vmem((3,) + ext, f32),

time: 32.2 us -> 32 us (level)
  no operation moved by 1% of the time
where the time goes in v4:
time: 32 us; the launch traced here: 31.8 us
  Pallas kernels  31.2 us (98%)
  between operations  0.64 us (2%)
    pallas_call x1, Pallas kernels, body(): pl.pallas_call(functools.partial(kernel, nx, ny), out_shape=(vmem((19,) +...  30 us
    pallas_call x1, Pallas kernels, body(): pl.pallas_call(closing, out_shape=tuple((jax.ShapeDtypeStruct(v.shape, f3...  1.19 us

profile of v4, /device:TPU:0, one launch (start us, length us, event | category | flops | bytes accessed | tf_op | source)
XLA Modules:
  0.0 31.8 jit_solution(6657720163178615186)
XLA Ops:
  0.6 30.0 %shard_map.85 = (f32[19,8,16,128]{3,2,1,0:T(8,128)S(1)}, f32[2,8,16,128]{3,2,1,0:T(8,128)S(1)}, f32[8,16,128]{2,1,0:T(8,128)S(1)}) custom-call(f32[8]{0:T(128)} %table_hbm.1, f32[19]{0:T(128)} %rates_hbm.1, f32[19,8,16,128]{3,2,1,0:T(8,128)} %pops_hbm.1, s32[8,16,128]{2,1,0:T(8,128)} %mask_hbm.1, s32[8,16,128]{2,1,0:T(8,128)} %class_hbm.1, ...), custom_call_target="tpu_custom_call" | custom-call | tf_op jit(solution)/shard_map/pallas_call | solution.py:789
  30.6 1.2 %shard_map.86 = (f32[19,8,16,128]{3,2,1,0:T(8,128)}, f32[2,8,16,128]{3,2,1,0:T(8,128)}, f32[8,16,128]{2,1,0:T(8,128)}) custom-call(f32[19,8,16,128]{3,2,1,0:T(8,128)S(1)} %get-tuple-element.6.adjoint, f32[2,8,16,128]{3,2,1,0:T(8,128)S(1)} %get-tuple-element.7.density, f32[8,16,128]{2,1,0:T(8,128)S(1)} %get-tuple-element.8.wet), custom_call_target="tpu_custom_call" | custom-call | tf_op jit(solution)/shard_map/pallas_call | solution.py:824

commit v5 on v4

--- a/solution.py
+++ b/solution.py
@@ -564,11 +564,11 @@
         unpack(r0, k, 0, psi_ext)
     for part in (Column(0), Column(B - 1)):
         forward(part)
-    finish(first, ACROSS)
-    for k in ACROSS:
-        unpack(r0, k, 0, psi_ext)
     second = {}
     for pair, ends in ((PAIR_A, ENDS_A), (PAIR_B, ENDS_B)):
+        finish(first, pair)
+        for k in pair:
+            unpack(r0, k, 0, psi_ext)
         for x, y in ends:
             forward(Row(x, y, B // 2))
         for k in pair:

time: 32 us -> 32 us (level)
  no operation moved by 1% of the time
where the time goes in v5:
time: 32 us; the launch traced here: 31.8 us
  Pallas kernels  31.2 us (98%)
  between operations  0.64 us (2%)
    pallas_call x1, Pallas kernels, body(): pl.pallas_call(functools.partial(kernel, nx, ny), out_shape=(vmem((19,) +...  30 us
    pallas_call x1, Pallas kernels, body(): pl.pallas_call(closing, out_shape=tuple((jax.ShapeDtypeStruct(v.shape, f3...  1.19 us

profile of v5, /device:TPU:0, one launch (start us, length us, event | category | flops | bytes accessed | tf_op | source)
XLA Modules:
  0.0 31.8 jit_solution(13596958612294865041)
XLA Ops:
  0.6 30.0 %shard_map.85 = (f32[19,8,16,128]{3,2,1,0:T(8,128)S(1)}, f32[2,8,16,128]{3,2,1,0:T(8,128)S(1)}, f32[8,16,128]{2,1,0:T(8,128)S(1)}) custom-call(f32[8]{0:T(128)} %table_hbm.1, f32[19]{0:T(128)} %rates_hbm.1, f32[19,8,16,128]{3,2,1,0:T(8,128)} %pops_hbm.1, s32[8,16,128]{2,1,0:T(8,128)} %mask_hbm.1, s32[8,16,128]{2,1,0:T(8,128)} %class_hbm.1, ...), custom_call_target="tpu_custom_call" | custom-call | tf_op jit(solution)/shard_map/pallas_call | solution.py:789
  30.6 1.2 %shard_map.86 = (f32[19,8,16,128]{3,2,1,0:T(8,128)}, f32[2,8,16,128]{3,2,1,0:T(8,128)}, f32[8,16,128]{2,1,0:T(8,128)}) custom-call(f32[19,8,16,128]{3,2,1,0:T(8,128)S(1)} %get-tuple-element.6.adjoint, f32[2,8,16,128]{3,2,1,0:T(8,128)S(1)} %get-tuple-element.7.density, f32[8,16,128]{2,1,0:T(8,128)S(1)} %get-tuple-element.8.wet), custom_call_target="tpu_custom_call" | custom-call | tf_op jit(solution)/shard_map/pallas_call | solution.py:824
